TPU v7x, 512 devices: a whole 4x4x16 slice. The times are simulated.
512 devices in a mesh: replica: 4 (over x), fsdp: 16 (over z), tensor: 8 (over y, core).
Axes of the slice: x: 4, y: 4, z: 16, core: 2. Of those that a mesh axis runs over, the one named last changes fastest.
Arguments:
- momentum: float32 [4, 4096, 14336], P('replica', 'fsdp', 'tensor'), may hold values from -600 to 600
- gradient: bfloat16 [4, 4096, 14336], P('replica', 'fsdp', 'tensor'), may hold values from -300 to 300
- right_in: float32 [14336, 256], P(('tensor', 'fsdp')), may hold values from -6 to 6
Outputs:
- left_factor: float32 [4096, 256], P('fsdp')
- right_factor: float32 [14336, 256], P(('tensor', 'fsdp'))
- new_momentum: float32 [4, 4096, 14336], P('replica', 'fsdp', 'tensor')
All inputs are finite; a program needn't handle non-finite values.
Results may differ from a plain program's by a relative error of at most 0.0003.
Values sent between devices are 32-bit elements; how exact they have to be, the bound alone decides.
No kernel may reach another device: no remote copies, remote signals or barrier semaphores. Data moves between devices by JAX's collectives and lax.ppermute only.
A program may use at most 64 MiB of HBM per device.

v0:
```python
import math

import jax
import jax.numpy as jnp
from jax import lax
from jax.sharding import PartitionSpec as P


def shards(momentum, gradient, right_in):
    highest = lax.Precision.HIGHEST
    buffer = momentum[0] + gradient[0].astype(jnp.float32)
    row_count = buffer.shape[0]
    col_count = buffer.shape[1]
    replicas = lax.axis_size("replica")
    fsdp_count = lax.axis_size("fsdp")
    tensor_count = lax.axis_size("tensor")
    col_share = col_count // fsdp_count
    partial_value = jnp.dot(
        buffer, lax.all_gather(right_in, "fsdp", axis=0, tiled=True), precision=highest
    )
    partial_value = partial_value / replicas
    projected = lax.psum(partial_value, ("replica", "tensor"))
    gram_matrix = lax.psum(jnp.dot(projected.T, projected, precision=highest), "fsdp")
    factor_low = jnp.linalg.cholesky(gram_matrix)
    orthonormal = jax.scipy.linalg.solve_triangular(factor_low, projected.T, lower=True).T
    back_terms = jnp.dot(buffer.T, orthonormal, precision=highest) / replicas
    back_proj = lax.psum(back_terms, ("replica", "fsdp"))
    squares = lax.psum(jnp.sum(back_proj * back_proj, axis=0), "tensor")
    own_rows = lax.dynamic_slice_in_dim(back_proj, lax.axis_index("fsdp") * col_share, col_share, 0)
    column_norm = jnp.sqrt(squares + 1e-06)
    right_factor = own_rows * (math.sqrt(col_count * tensor_count) / column_norm)[None, :]
    left_factor = orthonormal * math.sqrt(row_count * fsdp_count)
    new_momentum = buffer - 0.1 * jnp.dot(orthonormal, back_proj.T, precision=highest)
    return (left_factor, right_factor, new_momentum[None])


def solution(mesh):
    placed = (
        P("replica", "fsdp", "tensor"),
        P("replica", "fsdp", "tensor"),
        P(("tensor", "fsdp"), None),
    )
    return jax.shard_map(
        shards,
        mesh=mesh,
        in_specs=placed,
        out_specs=(P("fsdp", None), P(("tensor", "fsdp"), None), P("replica", "fsdp", "tensor")),
        check_vma=False,
    )
```

profile of v0, /device:TPU:1, one launch (start us, length us, event | category | flops | bytes accessed | tf_op | source)
XLA Modules:
  0.0 737.2 jit_solution(18388604268223584464)
XLA Ops:
  7.9 71.2 %all-gather.2.cloned.1.call-done = f32[1792,256]{1,0:T(8,128)} async-done(((f32[112,256]{1,0:T(8,128)}), f32[1792,256]{1,0:T(8,128)}) %all-gather.2.cloned.1.call-update) | async-done | bytes 1835024 | tf_op jit(solution)/shard_map/all_gather | solution.py:19
  79.2 4.8 fusion.5
  84.1 138.1 %all-reduce.5.cloned.1.call-done = f32[256,256]{1,0:T(8,128)} async-done(((f32[256,256]{1,0:T(8,128)}), f32[256,256]{1,0:T(8,128)}) %all-reduce.5.cloned.1.call-update) | async-done | bytes 262160 | tf_op jit(solution)/shard_map/psum | solution.py:22
  222.2 2.3 fusion.19
  224.8 126.6 %all-reduce.7.cloned.1.call-done = f32[256,256]{0,1:T(8,128)} async-done(((f32[256,256]{0,1:T(8,128)}), f32[256,256]{0,1:T(8,128)}) %all-reduce.7.cloned.1.call-update) | async-done | bytes 262160 | tf_op jit(solution)/shard_map/psum | solution.py:23
  351.3 1.1 copy.7
  352.4 1.0 fusion.8
  353.5 11.7 %cholesky.50 = f32[128,128]{1,0:T(8,128)S(1)} custom-call(f32[128,128]{1,0:T(8,128)S(1)} %cholesky.118), custom_call_target="Cholesky" | custom-call | tf_op jit(solution)/shard_map/jit(cholesky)/cholesky | solution.py:24
  365.9 10.4 %custom-call.15 = f32[1,128,128]{1,2,0:T(8,128)} custom-call(f32[1,128,128]{2,1,0:T(8,128)S(1)} %get-tuple-element.27), custom_call_target="InvertDiagBlocksLowerTriangular" | custom-call | tf_op jit(solution)/shard_map/jit(cholesky)/cholesky | solution.py:24
  376.3 0.9 cholesky.113
  377.2 1.0 constant_dynamic-update-slice_fusion
  378.2 0.9 convolution_subtract_fusion.1
  379.1 12.5 %cholesky.105 = f32[128,128]{1,0:T(8,128)S(1)} custom-call(f32[128,128]{1,0:T(8,128)} %convolution_subtract_fusion.1), custom_call_target="Cholesky" | custom-call | tf_op jit(solution)/shard_map/jit(cholesky)/cholesky | solution.py:24
  393.8 5.4 while.1
  394.5 2.0 bitcast_dynamic-update-slice_fusion.2
  397.1 2.0 bitcast_dynamic-update-slice_fusion.2
  399.2 20.5 %custom-call.16 = f32[2,128,128]{1,2,0:T(8,128)S(1)} custom-call(f32[2,128,128]{2,1,0:T(8,128)} %get-tuple-element.10), custom_call_target="InvertDiagBlocksLowerTriangular" | custom-call | tf_op jit(solution)/shard_map/jit(_solve_triangular)/triangular_solve | solution.py:25
  420.7 4.3 convolution_multiply_fusion.1
  425.0 0.8 copy.8
  425.9 274.0 %all-reduce.9.cloned.1.call-done = f32[1792,256]{1,0:T(8,128)} async-done(((f32[1792,256]{1,0:T(8,128)}), f32[1792,256]{1,0:T(8,128)}) %all-reduce.9.cloned.1.call-update) | async-done | bytes 1835024 | tf_op jit(solution)/shard_map/psum | solution.py:27
  699.9 1.8 multiply_reduce_fusion
  701.7 21.6 %psum.31 = f32[256]{0:T(256)S(1)} all-reduce(f32[256]{0:T(256)S(1)} %multiply_reduce_fusion), channel_id=1, replica_groups=mesh['replica'=4,'fsdp'=16,'tensor'=8] {'tensor'}, use_global_device_ids=true, to_apply=%region_8.9 | all-reduce | flops 256 | bytes 2048 | tf_op jit(solution)/shard_map/psum | solution.py:28
  723.3 5.8 fusion.1
  729.1 1.6 dynamic-slice_multiply_fusion
  (33 shorter events, 4.7 us)
Async XLA Ops:
  7.2 72.0 %all-gather.2.cloned.1.call-start = ((), (), s32[]{:S(2)}) async-start(), calls=%async_computation | async-start | bytes 1949696 | tf_op jit(solution)/shard_map/all_gather | solution.py:19
  7.9 214.3 %all-reduce.5.cloned.1.call-start = ((), (), s32[]{:S(2)}) async-start(), calls=%async_computation.1 | async-start | bytes 524288 | tf_op jit(solution)/shard_map/psum | solution.py:22
  84.0 267.3 %all-reduce.7.cloned.1.call-start = ((), (), s32[]{:S(2)}) async-start(), calls=%async_computation.2 | async-start | bytes 524288 | tf_op jit(solution)/shard_map/psum | solution.py:23
  224.5 475.4 %all-reduce.9.cloned.1.call-start = ((), (), s32[]{:S(2)}) async-start(), calls=%async_computation.3 | async-start | bytes 3670016 | tf_op jit(solution)/shard_map/psum | solution.py:27
  352.4 67.2 %copy-start.2 = (f32[256,256]{1,0:T(8,128)S(1)}, f32[256,256]{1,0:T(8,128)}, u32[]{:S(2)}) copy-start(f32[256,256]{1,0:T(8,128)} %all-reduce.5.cloned.1.call-done) | copy-start | bytes 786436
  353.5 67.2 %copy-start = (f32[1,256,1792]{2,1,0:T(8,128)S(1)}, f32[1,256,1792]{2,1,0:T(8,128)}, u32[]{:S(2)}) copy-start(f32[1,256,1792]{2,1,0:T(8,128)} %param.3) | copy-start | bytes 5505028
  353.5 67.2 %copy-start.1 = (bf16[1,256,1792]{2,1,0:T(8,128)(2,1)S(1)}, bf16[1,256,1792]{2,1,0:T(8,128)(2,1)}, u32[]{:S(2)}) copy-start(bf16[1,256,1792]{2,1,0:T(8,128)(2,1)} %param.4) | copy-start | bytes 2752516
  365.2 0.6 copy-start.3
Sparse Core Ops, SparseCore 0:
  10.1 69.0 all-gather.1
  84.1 138.0 all-reduce.4
  225.2 126.1 all-reduce.6
  425.1 274.7 all-reduce.8
where the time goes:
time: 738 us; the launch traced here: 737 us
  waiting for transfers between devices  611 us (83%)
  other arithmetic  60.3 us (8%)
  blocking collectives  21.6 us (3%)
  matrix products  20.2 us (3%)
  between operations  15.2 us (2%)
  local copies, waits for them, and re-layouts  8.67 us (1%)
    psum x1, waiting for transfers between devices, shards(): back_proj = lax.psum(back_terms, ('replica', 'fsdp'))  274 us
    psum x1, waiting for transfers between devices, shards(): projected = lax.psum(partial_value, ('replica', 'tensor'))  138 us
    psum x1, waiting for transfers between devices, shards(): lax.psum(jnp.dot(projected.T, projected, precision=highest), 'fsdp')  127 us
    all_gather x1, waiting for transfers between devices, shards(): lax.all_gather(right_in, 'fsdp', axis=0, tiled=True)  71.2 us
    another operation x6, other arithmetic, shards(): factor_low = jnp.linalg.cholesky(gram_matrix)  35.4 us
    psum x1, blocking collectives, shards(): squares = lax.psum(jnp.sum(back_proj * back_proj, axis=0), 'tensor')  21.6 us
    another operation x3, other arithmetic, shards(): jax.scipy.linalg.solve_triangular(factor_low, projected.T, lower=True)  20.5 us
  transfers between devices with their start and end apart: 4, of which 4 were waited for; matrix products, arithmetic and copies ran while one was open for 0% of the time, Pallas kernels for 0%

commit v1 on v0

v1 whole, which is shorter than its diff:
```python
import math

import jax
import jax.numpy as jnp
from jax import lax
from jax.sharding import PartitionSpec as P

HIGHEST = lax.Precision.HIGHEST
GROUP = ("replica", "tensor")


def spread(block, axes, count):
    copies = jnp.broadcast_to(block[None], (count,) + block.shape)
    return lax.all_to_all(copies, axes, 0, 0, tiled=True)


def inverse_factor(gram_matrix):
    factor_low = jnp.linalg.cholesky(gram_matrix)
    unit = jnp.eye(gram_matrix.shape[0], dtype=jnp.float32)
    return jax.scipy.linalg.solve_triangular(factor_low, unit, lower=True)


def shards(momentum, gradient, right_in):
    buffer = momentum[0] + gradient[0].astype(jnp.float32)
    row_count, col_count = buffer.shape
    rank = right_in.shape[1]
    replicas = lax.axis_size("replica")
    fsdp_count = lax.axis_size("fsdp")
    tensor_count = lax.axis_size("tensor")
    group_count = replicas * tensor_count
    replica = lax.axis_index("replica")
    place = replica * tensor_count + lax.axis_index("tensor")
    own = right_in.shape[0]
    piece = own // replicas
    quarter = piece * fsdp_count
    slab = rank // group_count
    band = row_count // group_count

    right_piece = lax.dynamic_slice_in_dim(right_in, replica * piece, piece, 0)
    right_quarter = spread(right_piece, "fsdp", fsdp_count).reshape(quarter, rank)
    turned = buffer.T.reshape(fsdp_count, replicas, piece, row_count)
    turned = turned.transpose(1, 0, 2, 3).reshape(col_count, row_count)
    mean_quarter = lax.psum_scatter(turned, "replica", scatter_dimension=0, tiled=True) / replicas

    partial_value = lax.dot_general(
        mean_quarter, right_quarter, (((0,), (0,)), ((), ())), precision=HIGHEST
    )
    partial_value = partial_value.reshape(group_count, band, rank)
    partial_value = lax.all_to_all(partial_value, GROUP, 0, 0, tiled=True)
    projected = spread(jnp.sum(partial_value, axis=0), GROUP, group_count).reshape(row_count, rank)

    gram_terms = lax.dot_general(projected, projected, (((0,), (0,)), ((), ())), precision=HIGHEST)
    gram_slab = lax.dynamic_slice_in_dim(gram_terms, place * slab, slab, 0)
    raw_terms = jnp.dot(mean_quarter, projected, precision=HIGHEST)
    terms = jnp.concatenate(
        [
            raw_terms.reshape(fsdp_count, piece, rank),
            jnp.broadcast_to(gram_slab[None], (fsdp_count, slab, rank)),
        ],
        axis=1,
    )
    sums = jnp.sum(lax.all_to_all(terms, "fsdp", 0, 0, tiled=True), axis=0)
    raw_own, gram_slab = sums[:piece], sums[piece:]
    raw_quarter = spread(raw_own, "fsdp", fsdp_count).reshape(quarter, rank)
    gram_matrix = spread(gram_slab, GROUP, group_count).reshape(rank, rank)

    inverse = inverse_factor(gram_matrix)
    orthonormal = jnp.dot(projected, inverse.T, precision=HIGHEST)
    back_quarter = jnp.dot(raw_quarter, inverse.T, precision=HIGHEST)
    back = lax.all_gather(back_quarter, "replica", axis=0, tiled=False)
    squares = jnp.sum(back_quarter * back_quarter, axis=0)[None]
    squares = jnp.sum(spread(squares, GROUP, group_count), axis=(0, 1))
    back = back.reshape(replicas, fsdp_count, piece, rank).transpose(1, 0, 2, 3)
    column_norm = jnp.sqrt(squares + 1e-06)
    own_rows = lax.dynamic_index_in_dim(back, lax.axis_index("fsdp"), 0, False).reshape(own, rank)
    right_factor = own_rows * (math.sqrt(col_count * tensor_count) / column_norm)[None, :]
    left_factor = orthonormal * math.sqrt(row_count * fsdp_count)
    back = back.reshape(col_count, rank)
    new_momentum = buffer - 0.1 * jnp.dot(orthonormal, back.T, precision=HIGHEST)
    return (left_factor, right_factor, new_momentum[None])


def solution(mesh):
    placed = (
        P("replica", "fsdp", "tensor"),
        P("replica", "fsdp", "tensor"),
        P(("tensor", "fsdp"), None),
    )
    return jax.shard_map(
        shards,
        mesh=mesh,
        in_specs=placed,
        out_specs=(P("fsdp", None), P(("tensor", "fsdp"), None), P("replica", "fsdp", "tensor")),
        check_vma=False,
    )
```

time: 738 us -> 272 us (0.37)
  waiting for transfers between devices: 611 us -> 48.4 us
  blocking collectives: 21.6 us -> 99.8 us
  starting transfers between devices: 0.34 us -> 18.4 us
  local copies, waits for them, and re-layouts: 8.67 us -> 20.8 us
  matrix products: 20.2 us -> 10.1 us
    psum x3 -> x0, waiting for transfers between devices: 539 us -> none  [the longest x1 274 us: shards(): back_proj = lax.psum(back_terms, ('replica', 'fsdp'))]
    all_to_all x0 -> x3, blocking collectives: none -> 99.8 us  [the longest x1 40.5 us: shards(): sums = jnp.sum(lax.all_to_all(terms, 'fsdp', 0, 0, tiled=True), axis=0)]
    all_gather x1, waiting for transfers between devices: 71.2 us -> 21.9 us  [shards(): back = lax.all_gather(back_quarter, 'replica', axis=0, tiled=False)]
    all_to_all x0 -> x4, waiting for transfers between devices: none -> 24.3 us  [spread(): return lax.all_to_all(copies, axes, 0, 0, tiled=True)]
    psum x1 -> x0, blocking collectives: 21.6 us -> none  [shards(): squares = lax.psum(jnp.sum(back_proj * back_proj, axis=0), 'tensor')]
    all_to_all x0 -> x4, starting transfers between devices: none -> 18.2 us  [spread(): return lax.all_to_all(copies, axes, 0, 0, tiled=True)]
    reshape x0 -> x8, local copies, waits for them, and re-layouts: none -> 8.72 us  [the longest x1 2.77 us: shards(): back = back.reshape(col_count, rank)]
    dot_general x4 -> x6, matrix products: 17.2 us -> 8.77 us  [the longest x1 4.51 us: shards(): jnp.dot(orthonormal, back.T, precision=HIGHEST)]
  transfers between devices with their start and end apart: 4 -> 6, of which waited for: 4 -> 5; matrix products, arithmetic and copies ran while one was open for 0% -> 23% of each run, Pallas kernels for 0% -> 0%
where the time goes in v1:
time: 272 us; the launch traced here: 271 us
  blocking collectives  99.8 us (37%)
  other arithmetic  57.6 us (21%)
  waiting for transfers between devices  48.4 us (18%)
  local copies, waits for them, and re-layouts  20.8 us (8%)
  starting transfers between devices  18.4 us (7%)
  between operations  15.7 us (6%)
  matrix products  10.1 us (4%)
    all_to_all x1, blocking collectives, shards(): sums = jnp.sum(lax.all_to_all(terms, 'fsdp', 0, 0, tiled=True), axis=0)  40.5 us
    all_to_all x1, blocking collectives, spread(): return lax.all_to_all(copies, axes, 0, 0, tiled=True)  38.4 us
    another operation x6, other arithmetic, inverse_factor(): factor_low = jnp.linalg.cholesky(gram_matrix)  34 us
    all_to_all x4, waiting for transfers between devices, spread(): return lax.all_to_all(copies, axes, 0, 0, tiled=True)  24.3 us
    all_gather x1, waiting for transfers between devices, shards(): back = lax.all_gather(back_quarter, 'replica', axis=0, tiled=False)  21.9 us
    all_to_all x1, blocking collectives, shards(): partial_value = lax.all_to_all(partial_value, GROUP, 0, 0, tiled=True)  20.9 us
    another operation x3, other arithmetic, inverse_factor(): return jax.scipy.linalg.solve_triangular(factor_low, unit, lower=True)  19.7 us
    all_to_all x4, starting transfers between devices, spread(): return lax.all_to_all(copies, axes, 0, 0, tiled=True)  18.2 us
  transfers between devices with their start and end apart: 6, of which 5 were waited for; matrix products, arithmetic and copies ran while one was open for 23% of the time, Pallas kernels for 0%

profile of v1, /device:TPU:1, one launch (start us, length us, event | category | flops | bytes accessed | tf_op | source)
XLA Modules:
  0.0 271.2 jit_solution(16177690292825543693)
XLA Ops:
  7.2 1.9 fusion.2
  9.1 1.7 copy.34
  10.8 1.5 reshape.74
  13.9 2.6 reshape.75
  16.6 38.4 %all_to_all.35 = f32[16,28,256]{2,1,0:T(8,128)S(1)} all-to-all(f32[16,28,256]{2,1,0:T(8,128)S(1)} %broadcast_in_dim.15), channel_id=1, replica_groups=mesh['replica'=4,'fsdp'=16,'tensor'=8] {'fsdp'}, dimensions={0} | all-to-all | bytes 917504 | tf_op jit(solution)/shard_map/all_to_all | solution.py:14
  55.0 2.2 reduce-scatter.2.cloned.1.call-done
  59.1 20.9 %all_to_all.36 = f32[32,8,256]{2,1,0:T(8,128)S(1)} all-to-all(f32[32,8,256]{2,1,0:T(8,128)S(1)} %fusion.3), channel_id=1, replica_groups=mesh['replica'=4,'fsdp'=16,'tensor'=8] {'replica','tensor'}, dimensions={0} | all-to-all | bytes 524288 | tf_op jit(solution)/shard_map/all_to_all | solution.py:49
  80.8 3.7 %all-to-all-start.2 = ((f32[32,8,256]{2,1,0:T(8,128)}), f32[32,8,256]{2,1,0:T(8,128)S(1)}, u32[]{:S(2)}, u32[]{:S(2)}) async-start(f32[32,8,256]{2,1,0:T(8,128)} %broadcast_in_dim.16), calls=%async_computation.3 | async-start | bytes 524288 | tf_op jit(solution)/shard_map/all_to_all | solution.py:14
  84.6 9.0 %all-to-all-done.2 = f32[32,8,256]{2,1,0:T(8,128)S(1)} async-done(((f32[32,8,256]{2,1,0:T(8,128)}), f32[32,8,256]{2,1,0:T(8,128)S(1)}, u32[]{:S(2)}, u32[]{:S(2)}) %all-to-all-start.2) | async-done | bytes 262176 | tf_op jit(solution)/shard_map/all_to_all | solution.py:14
  94.9 40.5 %all_to_all.37 = f32[16,36,256]{2,1,0:T(8,128)S(1)} all-to-all(f32[16,36,256]{2,1,0:T(8,128)S(1)} %pad_maximum_fusion), channel_id=1, replica_groups=mesh['replica'=4,'fsdp'=16,'tensor'=8] {'fsdp'}, dimensions={0} | all-to-all | bytes 1179648 | tf_op jit(solution)/shard_map/all_to_all | solution.py:62
  136.2 6.1 %all-to-all-start.4 = ((f32[32,8,256]{2,1,0:T(8,128)}), f32[32,8,256]{2,1,0:T(8,128)S(1)}, u32[]{:S(2)}, u32[]{:S(2)}) async-start(f32[32,8,256]{2,1,0:T(8,128)} %broadcast_in_dim.18), calls=%async_computation.5 | async-start | bytes 524288 | tf_op jit(solution)/shard_map/all_to_all | solution.py:14
  142.5 9.0 %all-to-all-done.4 = f32[32,8,256]{2,1,0:T(8,128)S(1)} async-done(((f32[32,8,256]{2,1,0:T(8,128)}), f32[32,8,256]{2,1,0:T(8,128)S(1)}, u32[]{:S(2)}, u32[]{:S(2)}) %all-to-all-start.4) | async-done | bytes 262176 | tf_op jit(solution)/shard_map/all_to_all | solution.py:14
  152.3 4.3 %all-to-all-start.5 = ((f32[16,28,256]{2,1,0:T(8,128)}), f32[16,28,256]{2,1,0:T(8,128)S(1)}, u32[]{:S(2)}, u32[]{:S(2)}) async-start(f32[16,28,256]{2,1,0:T(8,128)} %broadcast_in_dim.19), calls=%async_computation.6 | async-start | bytes 1048576 | tf_op jit(solution)/shard_map/all_to_all | solution.py:14
  157.1 11.7 %cholesky.50 = f32[128,128]{1,0:T(8,128)S(1)} custom-call(f32[128,128]{1,0:T(8,128)S(1)} %cholesky.118), custom_call_target="Cholesky" | custom-call | tf_op jit(solution)/shard_map/jit(cholesky)/cholesky | solution.py:18
  168.9 9.8 %custom-call.15 = f32[1,128,128]{1,2,0:T(8,128)S(1)} custom-call(f32[1,128,128]{2,1,0:T(8,128)S(1)} %get-tuple-element.26), custom_call_target="InvertDiagBlocksLowerTriangular" | custom-call | tf_op jit(solution)/shard_map/jit(cholesky)/cholesky | solution.py:18
  179.2 11.7 %cholesky.105 = f32[128,128]{1,0:T(8,128)S(1)} custom-call(f32[128,128]{1,0:T(8,128)S(1)} %convolution_subtract_fusion.1), custom_call_target="Cholesky" | custom-call | tf_op jit(solution)/shard_map/jit(cholesky)/cholesky | solution.py:18
  193.1 4.3 %while.1 = (s32[]{:T(128)}, f32[256,256]{1,0:T(8,128)S(1)}, s32[2,2]{1,0:T(2,128)S(1)}, f32[2,128,128]{2,1,0:T(8,128)S(1)}, s32[]{:T(128)}) while((s32[]{:T(128)}, f32[256,256]{1,0:T(8,128)S(1)}, s32[2,2]{1,0:T(2,128)S(1)}, f32[2,128,128]{2,1,0:T(8,128)S(1)}, s32[]{:T(128)}) %tuple.30), condition=%wide.while_cond, body=%wide.while_body.sunk | while | flops 2 | bytes 131189 | solution.py:20
  197.4 19.7 %custom-call.16 = f32[2,128,128]{1,2,0:T(8,128)S(1)} custom-call(f32[2,128,128]{2,1,0:T(8,128)S(1)} %get-tuple-element.10), custom_call_target="InvertDiagBlocksLowerTriangular" | custom-call | tf_op jit(solution)/shard_map/jit(_solve_triangular)/triangular_solve | solution.py:20
  220.0 4.0 %all-to-all-start.6 = ((f32[32,1,256]{2,1,0:T(1,128)}), f32[32,1,256]{2,1,0:T(1,128)S(1)}, u32[]{:S(2)}, u32[]{:S(2)}) async-start(f32[32,1,256]{2,1,0:T(1,128)} %broadcast_in_dim.20), calls=%async_computation.7 | async-start | bytes 65536 | tf_op jit(solution)/shard_map/all_to_all | solution.py:14
  225.1 6.3 %all-to-all-done.6 = f32[32,1,256]{2,1,0:T(1,128)S(1)} async-done(((f32[32,1,256]{2,1,0:T(1,128)}), f32[32,1,256]{2,1,0:T(1,128)S(1)}, u32[]{:S(2)}, u32[]{:S(2)}) %all-to-all-start.6) | async-done | bytes 32800 | tf_op jit(solution)/shard_map/all_to_all | solution.py:14
  231.4 21.9 %all-gather.3.cloned.1.call-done = f32[1792,256]{1,0:T(8,128)} async-done(((f32[448,256]{1,0:T(8,128)}), f32[1792,256]{1,0:T(8,128)}) %all-gather.3.cloned.1.call-update) | async-done | bytes 1835024 | tf_op jit(solution)/shard_map/all_gather | solution.py:70
  253.3 1.5 reshape.80
  256.4 2.8 %reshape.82 = f32[1792,256]{1,0:T(8,128)} reshape(f32[16,4,28,256]{3,2,1,0:T(8,128)} %copy.39) | data formatting | bytes 3670016 | tf_op jit(solution)/shard_map/reshape | solution.py:78
  259.9 4.5 %fusion.1 = f32[1,256,1792]{2,1,0:T(8,128)} fusion(f32[256,256]{1,0:T(8,128)S(1)} %get-tuple-element.30, f32[1792,256]{1,0:T(8,128)} %reshape.82, f32[1,256,1792]{2,1,0:T(8,128)S(1)} %copy-done.1, bf16[1,256,1792]{2,1,0:T(8,128)(2,1)S(1)} %copy-done.2), kind=kOutput, calls=%fused_computation.4 | convolution fusion | flops 1411121152 | bytes 6684672 | tf_op jit(solution)/shard_map/dot_general | solution.py:79
  (64 shorter events, 19.4 us)
Async XLA Ops:
  7.2 9.3 %copy-start = (f32[112,256]{1,0:T(8,128)S(1)}, f32[112,256]{1,0:T(8,128)}, u32[]{:S(2)}) copy-start(f32[112,256]{1,0:T(8,128)} %param.5) | copy-start | bytes 344068
  7.2 50.0 %reduce-scatter.2.cloned.1.call-start = ((), (), s32[]{:S(2)}) async-start(), calls=%async_computation.8 | async-start | bytes 2293760 | tf_op jit(solution)/shard_map/reduce_scatter | solution.py:43
  80.8 12.8 %all-to-all-start.2 = ((f32[32,8,256]{2,1,0:T(8,128)}), f32[32,8,256]{2,1,0:T(8,128)S(1)}, u32[]{:S(2)}, u32[]{:S(2)}) async-start(f32[32,8,256]{2,1,0:T(8,128)} %broadcast_in_dim.16), calls=%async_computation.3 | async-start | bytes 524288 | tf_op jit(solution)/shard_map/all_to_all | solution.py:14
  136.2 15.3 %all-to-all-start.4 = ((f32[32,8,256]{2,1,0:T(8,128)}), f32[32,8,256]{2,1,0:T(8,128)S(1)}, u32[]{:S(2)}, u32[]{:S(2)}) async-start(f32[32,8,256]{2,1,0:T(8,128)} %broadcast_in_dim.18), calls=%async_computation.5 | async-start | bytes 524288 | tf_op jit(solution)/shard_map/all_to_all | solution.py:14
  152.3 65.6 %all-to-all-start.5 = ((f32[16,28,256]{2,1,0:T(8,128)}), f32[16,28,256]{2,1,0:T(8,128)S(1)}, u32[]{:S(2)}, u32[]{:S(2)}) async-start(f32[16,28,256]{2,1,0:T(8,128)} %broadcast_in_dim.19), calls=%async_computation.6 | async-start | bytes 1048576 | tf_op jit(solution)/shard_map/all_to_all | solution.py:14
  156.7 96.6 %all-gather.3.cloned.1.call-start = ((), (), s32[]{:S(2)}) async-start(), calls=%async_computation.9 | async-start | bytes 2293760 | tf_op jit(solution)/shard_map/all_gather | solution.py:70
  220.0 11.4 %all-to-all-start.6 = ((f32[32,1,256]{2,1,0:T(1,128)}), f32[32,1,256]{2,1,0:T(1,128)S(1)}, u32[]{:S(2)}, u32[]{:S(2)}) async-start(f32[32,1,256]{2,1,0:T(1,128)} %broadcast_in_dim.20), calls=%async_computation.7 | async-start | bytes 65536 | tf_op jit(solution)/shard_map/all_to_all | solution.py:14
  256.4 3.4 %copy-start.1 = (f32[1,256,1792]{2,1,0:T(8,128)S(1)}, f32[1,256,1792]{2,1,0:T(8,128)}, u32[]{:S(2)}) copy-start(f32[1,256,1792]{2,1,0:T(8,128)} %param.3) | copy-start | bytes 5505028
  256.4 3.4 %copy-start.2 = (bf16[1,256,1792]{2,1,0:T(8,128)(2,1)S(1)}, bf16[1,256,1792]{2,1,0:T(8,128)(2,1)}, u32[]{:S(2)}) copy-start(bf16[1,256,1792]{2,1,0:T(8,128)(2,1)} %param.4) | copy-start | bytes 2752516
Sparse Core Ops, SparseCore 0:
  16.6 40.5 reduce-scatter.1
  219.5 33.8 all-gather.2

commit v2 on v0

v2 whole, which is shorter than its diff:
```python
import functools
import math

import jax
import jax.numpy as jnp
from jax import lax
from jax.experimental import pallas as pl
from jax.experimental.pallas import tpu as pltpu
from jax.sharding import PartitionSpec as P

HIGHEST = lax.Precision.HIGHEST
GROUP = ("replica", "tensor")
PANEL = 64
NEAR = 4
LANES = 128
VMEM_LIMIT = 40 * 1024 * 1024
VMEM_WHOLE = 63 * 1024 * 1024


def exchange(blocks, axes, groups=None):
    return lax.all_to_all(blocks, axes, 0, 0, tiled=True, axis_index_groups=groups)


def pack(value):
    return jnp.concatenate([value[:, :LANES], value[:, LANES:]], axis=0)


def unpack(value):
    half = value.shape[0] // 2
    return jnp.concatenate([value[:half], value[half:]], axis=1)


def column_dot(left, right):
    return lax.dot_general(
        left, right, (((0,), (0,)), ((), ())), precision=HIGHEST, preferred_element_type=jnp.float32
    )


def row_dot(left, right):
    return lax.dot_general(
        left, right, (((1,), (1,)), ((), ())), precision=HIGHEST, preferred_element_type=jnp.float32
    )


def turn_kernel(where_ref, momentum_ref, gradient_ref, right_ref, *refs):
    outs, copies_ref, sorted_rows = refs[:-2], refs[-2], refs[-1]
    replica = where_ref[0]
    turned = (momentum_ref[0] + gradient_ref[0].astype(jnp.float32)).T
    replicas, blocks, packed = sorted_rows.shape[:3]
    piece = packed // 2
    for block in range(blocks):
        for part in range(replicas):
            start = (block * replicas + part) * piece
            rows = turned[start : start + piece, :]
            sorted_rows[part, block, :piece, :] = rows[:, :LANES]
            sorted_rows[part, block, piece:, :] = rows[:, LANES:]
    for step, out_ref in enumerate(outs):
        out_ref[...] = sorted_rows[lax.rem(replica + step, replicas)]

    @pl.when(pl.program_id(0) == 0)
    def _():
        rows = right_ref[:piece, :]
        for part in range(1, replicas):
            rows = jnp.where(replica == part, right_ref[part * piece : (part + 1) * piece, :], rows)
        copies_ref[...] = jnp.broadcast_to(pack(rows)[None], copies_ref.shape)


def turn(where, momentum, gradient, right_in, replicas, fsdp_count):
    row_count, col_count = momentum.shape[1:]
    own = col_count // fsdp_count
    group = math.lcm(own, LANES)
    steps = col_count // group
    packed = 2 * (own // replicas)
    block = (fsdp_count // steps, packed, LANES)
    whole = (fsdp_count, packed, LANES)
    return pl.pallas_call(
        turn_kernel,
        grid=(steps,),
        in_specs=[pl.BlockSpec(memory_space=pltpu.SMEM)]
        + [pl.BlockSpec((1, row_count, group), lambda i: (0, 0, i))] * 2
        + [pl.BlockSpec(right_in.shape, lambda i: (0, 0))],
        out_specs=[pl.BlockSpec(block, lambda i: (i, 0, 0))] * replicas
        + [pl.BlockSpec(whole, lambda i: (0, 0, 0))],
        out_shape=[jax.ShapeDtypeStruct(whole, jnp.float32)] * (replicas + 1),
        scratch_shapes=[pltpu.VMEM((replicas,) + block, jnp.float32)],
        compiler_params=pltpu.CompilerParams(vmem_limit_bytes=VMEM_WHOLE),
        name="turn",
    )(where, momentum, gradient, right_in)


def project_kernel(part_refs, right_ref, sum_ref, out_ref, right):
    blocks, packed = right_ref.shape[:2]
    piece = packed // 2
    for block in range(blocks):
        total = part_refs[0][block]
        for part_ref in part_refs[1:]:
            total = total + part_ref[block]
        rows = slice(block * piece, (block + 1) * piece)
        sum_ref[rows, :] = unpack(total)
        right[rows, :] = unpack(right_ref[block])
    out_ref[...] = column_dot(sum_ref[...], right[...])


def project(parts, right_quarter):
    def body(*refs):
        project_kernel(refs[: len(parts)], *refs[len(parts) :])

    blocks, packed, _ = right_quarter.shape
    quarter, rank = blocks * packed // 2, 2 * LANES
    return pl.pallas_call(
        body,
        out_shape=[
            jax.ShapeDtypeStruct((quarter, 2 * LANES), jnp.float32),
            jax.ShapeDtypeStruct((2 * LANES, rank), jnp.float32),
        ],
        scratch_shapes=[pltpu.VMEM((quarter, rank), jnp.float32)],
        compiler_params=pltpu.CompilerParams(vmem_limit_bytes=VMEM_LIMIT),
        name="project",
    )(*parts, right_quarter)


def sum_copies_kernel(scale, blocks_ref, out_ref):
    total = jnp.sum(blocks_ref[...], axis=0, keepdims=True) * scale
    out_ref[...] = jnp.broadcast_to(total, out_ref.shape)


def sum_copies(blocks, scale):
    return pl.pallas_call(
        functools.partial(sum_copies_kernel, scale),
        out_shape=jax.ShapeDtypeStruct(blocks.shape, jnp.float32),
        compiler_params=pltpu.CompilerParams(vmem_limit_bytes=VMEM_LIMIT),
        name="sum_copies",
    )(blocks)


def sum_kernel(blocks_ref, out_ref):
    rows = out_ref.shape[1]
    for receiver in range(out_ref.shape[0]):
        part = slice(receiver * rows, (receiver + 1) * rows)
        total = blocks_ref[0, part, :]
        for sender in range(1, blocks_ref.shape[0]):
            total = total + blocks_ref[sender, part, :]
        out_ref[receiver] = total


def sum_blocks(blocks, receivers):
    rows = blocks.shape[1] // receivers
    return pl.pallas_call(
        sum_kernel,
        out_shape=jax.ShapeDtypeStruct((receivers, rows, LANES), jnp.float32),
        compiler_params=pltpu.CompilerParams(vmem_limit_bytes=VMEM_LIMIT),
        name="sum_blocks",
    )(blocks)


def terms_kernel(share, where_ref, sum_ref, projected_ref, out_ref, gram):
    near, far, packed = out_ref.shape[:3]
    blocks = near * far
    piece = sum_ref.shape[0] // blocks
    slab = share * blocks
    projected = projected_ref[...]
    gram[...] = column_dot(projected, projected)
    rows = gram[pl.ds(pl.multiple_of(where_ref[2] * slab, slab), slab), :]
    raw = jnp.dot(
        sum_ref[...], projected, precision=HIGHEST, preferred_element_type=jnp.float32
    )
    rest = jnp.zeros((packed - 2 * (piece + share), LANES), jnp.float32)
    for block in range(blocks):
        a, b = divmod(block, near)
        out_ref[b, a, : 2 * piece, :] = pack(raw[block * piece : (block + 1) * piece, :])
        tail = pack(rows[block * share : (block + 1) * share, :])
        out_ref[b, a, 2 * piece :, :] = jnp.concatenate([tail, rest], axis=0)


def make_terms(where, column_sum, projected, blocks, tensor_count):
    rank = projected.shape[1]
    share = rank // tensor_count // blocks
    packed = 2 * (column_sum.shape[0] // blocks + share)
    whole = pl.BlockSpec(memory_space=pltpu.VMEM)
    return pl.pallas_call(
        functools.partial(terms_kernel, share),
        in_specs=[pl.BlockSpec(memory_space=pltpu.SMEM), whole, whole],
        out_specs=whole,
        out_shape=jax.ShapeDtypeStruct((NEAR, blocks // NEAR, -(-packed // 8) * 8, LANES), jnp.float32),
        scratch_shapes=[pltpu.VMEM((rank, rank), jnp.float32)],
        compiler_params=pltpu.CompilerParams(vmem_limit_bytes=VMEM_LIMIT),
        name="terms",
    )(where, column_sum, projected)


def slab_kernel(packed, sums_ref, slab_ref):
    near, far = sums_ref.shape[:2]
    share = slab_ref.shape[1] // (near * far)
    tail = slice(packed, packed + 2 * share)
    rows = [unpack(sums_ref[b, a, tail, :]) for a in range(far) for b in range(near)]
    slab_ref[...] = jnp.broadcast_to(jnp.concatenate(rows, axis=0)[None], slab_ref.shape)


def take_slab(sums, packed, slab, tensor_count):
    return pl.pallas_call(
        functools.partial(slab_kernel, packed),
        out_shape=jax.ShapeDtypeStruct((tensor_count, slab, 2 * LANES), jnp.float32),
        compiler_params=pltpu.CompilerParams(vmem_limit_bytes=VMEM_LIMIT),
        name="slab",
    )(sums)


def raw_kernel(sums_ref, raw_ref):
    near = sums_ref.shape[0]
    for block in range(raw_ref.shape[0]):
        a, b = divmod(block, near)
        raw_ref[block] = sums_ref[b, a, : raw_ref.shape[1], :]


def take_raw(sums, packed):
    near, far = sums.shape[:2]
    return pl.pallas_call(
        raw_kernel,
        out_shape=jax.ShapeDtypeStruct((near * far, packed, LANES), jnp.float32),
        compiler_params=pltpu.CompilerParams(vmem_limit_bytes=VMEM_LIMIT),
        name="raw",
    )(sums)


def invert_factor(work, inverse_ref):
    rank = work.shape[0]
    lane = lax.broadcasted_iota(jnp.int32, (PANEL, rank), 1)
    row = lax.broadcasted_iota(jnp.int32, (PANEL, rank), 0)
    lane8, row8 = lane[:8, :LANES], row[:8, :LANES]
    tiles = rank // LANES
    groups = PANEL // 8

    def every(value):
        return jnp.broadcast_to(value, (8, LANES))

    for panel in range(0, rank, PANEL):
        rows = [
            [
                work[panel + 8 * h : panel + 8 * h + 8, LANES * t : LANES * (t + 1)]
                for t in range(tiles)
            ]
            for h in range(groups)
        ]
        inverses = []
        for g in range(groups):
            tile, start = divmod(panel + 8 * g, LANES)
            shares = {
                h: [every(rows[h][tile][:, start + j : start + j + 1]) for j in range(8)]
                for h in range(g, groups)
            }
            pivot_rows = [[every(rows[g][t][j : j + 1]) for j in range(8)] for t in range(tiles)]
            pivot_inverses = None
            for k in range(8):
                inverse = 1.0 / every(shares[g][k][k : k + 1])
                if pivot_inverses is None:
                    pivot_inverses = inverse
                else:
                    pivot_inverses = jnp.where(row8 == k, inverse, pivot_inverses)
                pivot_row = [every(shares[g][j][k : k + 1]) for j in range(8)]
                for h in range(g, groups):
                    factor = shares[h][k] * inverse
                    if h == g:
                        factor = jnp.where(row8 > k, factor, 0.0)
                    for j in range(8):
                        if j != k:
                            shares[h][j] = shares[h][j] - factor * pivot_row[j]
                    shares[h][k] = jnp.where(row8 == k, 1.0, -factor) if h == g else -factor
            inverses.append(pivot_inverses)
            shares[g] = [jnp.where(row8 >= j, shares[g][j], 0.0) for j in range(8)]
            for h in range(groups - 1, g - 1, -1):
                for t in range(tiles):
                    products = [shares[h][j] * pivot_rows[t][j] for j in range(8)]
                    while len(products) > 1:
                        products = [a + b for a, b in zip(products[::2], products[1::2])]
                    total = products[0] if h == g else rows[h][t] + products[0]
                    if t == tile:
                        for j in range(8):
                            total = jnp.where(lane8 == start + j, shares[h][j], total)
                    rows[h][t] = total
        whole = jnp.concatenate([jnp.concatenate(r, axis=1) for r in rows], axis=0)
        scale = jnp.concatenate([jnp.concatenate([r] * tiles, axis=1) for r in inverses], axis=0)
        unit = jnp.where((lane > panel + row) & (lane < panel + PANEL), 0.0, whole)
        inverse_ref[panel : panel + PANEL, :] = jnp.where(lane <= panel + row, unit, 0.0) * jnp.sqrt(scale)
        below = panel + PANEL
        if below < rank:
            rest = work[below:, :]
            lanes = lax.broadcasted_iota(jnp.int32, rest.shape, 1)
            rest = jnp.where((lanes >= panel) & (lanes < below), 0.0, rest)
            first = below // LANES * LANES
            work[below:, :] = rest - column_dot((whole * scale)[:, first:], unit)[below - first :]


def factor_kernel(
    replicas, rows, gram_ref, projected_ref, raw_ref, inverse_ref, ortho_ref, left_ref, squares_ref, work, raw
):
    blocks, packed = raw_ref.shape[:2]
    piece = packed // 2
    for block in range(blocks):
        raw[block * piece : (block + 1) * piece, :] = unpack(raw_ref[block])
    work[...] = gram_ref[...]
    invert_factor(work, inverse_ref)
    inverse = inverse_ref[...]
    ortho = row_dot(projected_ref[...], inverse)
    ortho_ref[...] = jnp.dot(
        ortho, inverse, precision=HIGHEST, preferred_element_type=jnp.float32
    ) * (1.0 / replicas)
    left_ref[...] = ortho * math.sqrt(rows)
    inverse = inverse * (1.0 / replicas)
    inverse_ref[...] = inverse
    back = row_dot(raw[...], inverse)
    squares = pack(jnp.sum(back * back, axis=0, keepdims=True))
    rest = jnp.zeros((squares_ref.shape[1] - 2, LANES), jnp.float32)
    squares_ref[...] = jnp.broadcast_to(jnp.concatenate([squares, rest], axis=0)[None], squares_ref.shape)


def make_factor(gram_matrix, projected, raw_quarter, replicas, rows, group_count):
    rank = gram_matrix.shape[0]
    blocks, packed, _ = raw_quarter.shape
    return pl.pallas_call(
        functools.partial(factor_kernel, replicas, rows),
        out_shape=[
            jax.ShapeDtypeStruct(gram_matrix.shape, jnp.float32),
            jax.ShapeDtypeStruct(projected.shape, jnp.float32),
            jax.ShapeDtypeStruct(projected.shape, jnp.float32),
            jax.ShapeDtypeStruct((group_count, 8, LANES), jnp.float32),
        ],
        scratch_shapes=[
            pltpu.VMEM(gram_matrix.shape, jnp.float32),
            pltpu.VMEM((blocks * packed // 2, rank), jnp.float32),
        ],
        compiler_params=pltpu.CompilerParams(vmem_limit_bytes=VMEM_LIMIT),
        cost_estimate=pl.CostEstimate(flops=3 * 10**10, bytes_accessed=10**6, transcendentals=0),
        name="factor",
    )(gram_matrix, projected, raw_quarter)


def update_kernel(where_ref, momentum_ref, gradient_ref, ortho_ref, inverse_ref, *refs):
    parts, (out_ref, own_ref, sorted_rows, raw) = refs[:-4], refs[-4:]
    replicas, blocks, packed = sorted_rows.shape[:3]
    piece = packed // 2
    own = replicas * piece
    for step, part_ref in enumerate(parts):
        sorted_rows[lax.rem(where_ref[0] + step, replicas)] = part_ref[...]
    for block in range(blocks):
        for replica in range(replicas):
            start = block * own + replica * piece
            raw[start : start + piece, :] = unpack(sorted_rows[replica, block])
    correction = row_dot(ortho_ref[...], raw[...])
    out_ref[0] = momentum_ref[0] + gradient_ref[0].astype(jnp.float32) - 0.1 * correction

    @pl.when(where_ref[1] // blocks == pl.program_id(0))
    def _():
        start = pl.multiple_of(lax.rem(where_ref[1], blocks) * own, 8)
        own_ref[...] = row_dot(raw[pl.ds(start, own), :], inverse_ref[...])


def update(where, momentum, gradient, orthonormal, inverse, parts):
    row_count, own_count = momentum.shape[1:]
    replicas = len(parts)
    fsdp_count, packed, _ = parts[0].shape
    rank = orthonormal.shape[1]
    own = own_count // fsdp_count
    group = math.lcm(own, LANES)
    steps = own_count // group
    columns = pl.BlockSpec((1, row_count, group), lambda i: (0, 0, i))
    block = (fsdp_count // steps, packed, LANES)
    return pl.pallas_call(
        update_kernel,
        grid=(steps,),
        in_specs=[
            pl.BlockSpec(memory_space=pltpu.SMEM),
            columns,
            columns,
            pl.BlockSpec((row_count, rank), lambda i: (0, 0)),
            pl.BlockSpec((rank, rank), lambda i: (0, 0)),
        ]
        + [pl.BlockSpec(block, lambda i: (i, 0, 0))] * replicas,
        out_specs=[columns, pl.BlockSpec((own, rank), lambda i: (0, 0))],
        out_shape=[
            jax.ShapeDtypeStruct(momentum.shape, jnp.float32),
            jax.ShapeDtypeStruct((own, rank), jnp.float32),
        ],
        scratch_shapes=[
            pltpu.VMEM((replicas,) + block, jnp.float32),
            pltpu.VMEM((group, rank), jnp.float32),
        ],
        compiler_params=pltpu.CompilerParams(vmem_limit_bytes=VMEM_WHOLE),
        name="update",
    )(where, momentum, gradient, orthonormal, inverse, *parts)


def scale_kernel(columns, own_ref, squares_ref, out_ref):
    squares = unpack(jnp.sum(squares_ref[...], axis=0)[:2])
    out_ref[...] = own_ref[...] * (math.sqrt(columns) / jnp.sqrt(squares + 1e-06))


def make_right(own_rows, squares, columns):
    return pl.pallas_call(
        functools.partial(scale_kernel, columns),
        out_shape=jax.ShapeDtypeStruct(own_rows.shape, jnp.float32),
        compiler_params=pltpu.CompilerParams(vmem_limit_bytes=VMEM_LIMIT),
        name="scale",
    )(own_rows, squares)


def shards(momentum, gradient, right_in):
    row_count, col_count = momentum.shape[1:]
    rank = right_in.shape[1]
    replicas = lax.axis_size("replica")
    fsdp_count = lax.axis_size("fsdp")
    tensor_count = lax.axis_size("tensor")
    group_count = replicas * tensor_count
    where = jnp.stack([lax.axis_index("replica"), lax.axis_index("fsdp"), lax.axis_index("tensor")])
    band = row_count // group_count
    packed = 2 * (col_count // fsdp_count // replicas)
    slab = rank // tensor_count
    far = fsdp_count // NEAR
    near_groups = [[a * NEAR + b for b in range(NEAR)] for a in range(far)]
    far_groups = [[a * NEAR + b for a in range(far)] for b in range(NEAR)]

    def around(value, step):
        pairs = [(i, (i + step) % replicas) for i in range(replicas)]
        return lax.ppermute(value, "replica", pairs)

    *turned, right_copies = turn(where, momentum, gradient, right_in, replicas, fsdp_count)
    right_quarter = exchange(right_copies, "fsdp")
    parts = [turned[0]] + [around(turned[step], step) for step in range(1, replicas)]
    column_sum, partial_value = project(parts, right_quarter)

    partial_value = exchange(partial_value.reshape(group_count, band, rank), GROUP)
    projected = exchange(sum_copies(partial_value, 1.0 / replicas), GROUP).reshape(row_count, rank)

    terms = make_terms(where, column_sum, projected, fsdp_count, tensor_count)
    height = terms.shape[2]
    terms = exchange(terms.reshape(NEAR, far * height, LANES), "fsdp", near_groups)
    sums = exchange(sum_blocks(terms, far), "fsdp", far_groups)
    sums = exchange(sum_copies(sums, 1.0), "fsdp", far_groups).reshape(1, far * height, LANES)
    sums = exchange(jnp.broadcast_to(sums, (NEAR, far * height, LANES)), "fsdp", near_groups)
    sums = sums.reshape(NEAR, far, height, LANES)
    gram_matrix = exchange(take_slab(sums, packed, slab, tensor_count), "tensor").reshape(rank, rank)
    raw_quarter = take_raw(sums, packed)
    raw_parts = [raw_quarter] + [around(raw_quarter, -step) for step in range(1, replicas)]
    inverse, combined, left_factor, squares = make_factor(
        gram_matrix, projected, raw_quarter, replicas, row_count * fsdp_count, group_count
    )
    new_momentum, own_rows = update(where, momentum, gradient, combined, inverse, raw_parts)
    right_factor = make_right(own_rows, exchange(squares, GROUP), col_count * tensor_count)
    return (left_factor, right_factor, new_momentum)


def solution(mesh):
    placed = (
        P("replica", "fsdp", "tensor"),
        P("replica", "fsdp", "tensor"),
        P(("tensor", "fsdp"), None),
    )
    return jax.shard_map(
        shards,
        mesh=mesh,
        in_specs=placed,
        out_specs=(P("fsdp", None), P(("tensor", "fsdp"), None), P("replica", "fsdp", "tensor")),
        check_vma=False,
    )
```

time: 738 us -> 198 us (0.27)
  waiting for transfers between devices: 611 us -> 16.8 us
  blocking collectives: 21.6 us -> 97 us
  other arithmetic: 60.3 us -> 0.58 us
  starting transfers between devices: 0.34 us -> 52.8 us
  Pallas kernels: 0 us -> 23.9 us
  matrix products: 20.2 us -> 0 us
  between operations: 15.2 us -> 0.81 us
    psum x3 -> x0, waiting for transfers between devices: 539 us -> none  [the longest x1 274 us: shards(): back_proj = lax.psum(back_terms, ('replica', 'fsdp'))]
    all_to_all x0 -> x6, blocking collectives: none -> 97 us  [exchange(): lax.all_to_all(blocks, axes, 0, 0, tiled=True, axis_index_groups=groups)]
    all_gather x1 -> x0, waiting for transfers between devices: 71.2 us -> none  [shards(): lax.all_gather(right_in, 'fsdp', axis=0, tiled=True)]
    another operation x9 -> x1, other arithmetic: 55.9 us -> 0.58 us  [shards(): jnp.stack([lax.axis_index('replica'), lax.axis_index('fsdp'), lax.axis_in...]
    all_to_all x0 -> x3, starting transfers between devices: none -> 33.6 us  [exchange(): lax.all_to_all(blocks, axes, 0, 0, tiled=True, axis_index_groups=groups)]
    pallas_call x0 -> x11, Pallas kernels: none -> 23.9 us  [the longest x1 11.2 us: make_factor(): pl.pallas_call(functools.partial(factor_kernel, replicas, rows), out_shap...]
    psum x1 -> x0, blocking collectives: 21.6 us -> none  [shards(): squares = lax.psum(jnp.sum(back_proj * back_proj, axis=0), 'tensor')]
    ppermute x0 -> x6, starting transfers between devices: none -> 19.2 us  [around(): return lax.ppermute(value, 'replica', pairs)]
  transfers between devices with their start and end apart: 4 -> 9, of which waited for: 4 -> 4; matrix products, arithmetic and copies ran while one was open for 0% -> 0% of each run, Pallas kernels for 0% -> 9%
where the time goes in v2:
time: 198 us; the launch traced here: 197 us
  blocking collectives  97 us (49%)
  starting transfers between devices  52.8 us (27%)
  Pallas kernels  23.9 us (12%)
  waiting for transfers between devices  16.8 us (8%)
  local copies, waits for them, and re-layouts  4.95 us (2%)
    all_to_all x6, blocking collectives, exchange(): lax.all_to_all(blocks, axes, 0, 0, tiled=True, axis_index_groups=groups)  97 us
    all_to_all x3, starting transfers between devices, exchange(): lax.all_to_all(blocks, axes, 0, 0, tiled=True, axis_index_groups=groups)  33.6 us
    ppermute x6, starting transfers between devices, around(): return lax.ppermute(value, 'replica', pairs)  19.2 us
    ppermute x6, waiting for transfers between devices, around(): return lax.ppermute(value, 'replica', pairs)  16.6 us
    pallas_call x1, Pallas kernels, make_factor(): pl.pallas_call(functools.partial(factor_kernel, replicas, rows), out_shap...  11.2 us
    pallas_call x1, Pallas kernels, update(): pl.pallas_call(update_kernel, grid=(steps,), in_specs=[pl.BlockSpec(memor...  5.86 us
    unnamed x18, local copies, waits for them, and re-layouts  4.92 us
  transfers between devices with their start and end apart: 9, of which 4 were waited for; matrix products, arithmetic and copies ran while one was open for 0% of the time, Pallas kernels for 9%

profile of v2, /device:TPU:1, one launch (start us, length us, event | category | flops | bytes accessed | tf_op | source)
XLA Modules:
  0.0 196.8 jit_solution(12942906340118551071)
XLA Ops:
  1.2 3.3 %turn.1 = (f32[16,56,128]{2,1,0:T(8,128)}, f32[16,56,128]{2,1,0:T(8,128)}, f32[16,56,128]{2,1,0:T(8,128)}, f32[16,56,128]{2,1,0:T(8,128)}, f32[16,56,128]{2,1,0:T(8,128)}) custom-call(s32[3]{0:T(128)} %pad_add_fusion.where_ref, f32[1,256,1792]{2,1,0:T(8,128)} %momentum_ref.3, bf16[1,256,1792]{2,1,0:T(8,128)(2,1)} %gradient_ref.3, f32[112,256]{1,0:T(8,128)} %right_ref.1), custom_call_target="tpu_custom_call" | custom-call | tf_op jit(solution)/shard_map/turn/pallas_call | solution.py:76
  4.5 15.8 %all-to-all-start = ((f32[16,56,128]{2,1,0:T(8,128)}), f32[16,56,128]{2,1,0:T(8,128)S(1)}, u32[]{:S(2)}, u32[]{:S(2)}) async-start(f32[16,56,128]{2,1,0:T(8,128)} %get-tuple-element.20), calls=%async_computation | async-start | bytes 917504 | tf_op jit(solution)/shard_map/all_to_all | solution.py:21
  20.3 3.1 %collective-permute-start = (f32[16,56,128]{2,1,0:T(8,128)}, f32[16,56,128]{2,1,0:T(8,128)S(1)}, u32[]{:S(2)}, u32[]{:S(2)}) collective-permute-start(f32[16,56,128]{2,1,0:T(8,128)} %get-tuple-element.17), channel_id=1, source_target_pairs={{0,128},{128,256},{256,384},{384,0},{1,129},{129,257},{257,385},{3... | collective-permute-start | bytes 1376264 | tf_op jit(solution)/shard_map/ppermute | solution.py:423
  23.4 4.4 %collective-permute-start.1 = (f32[16,56,128]{2,1,0:T(8,128)}, f32[16,56,128]{2,1,0:T(8,128)S(1)}, u32[]{:S(2)}, u32[]{:S(2)}) collective-permute-start(f32[16,56,128]{2,1,0:T(8,128)} %get-tuple-element.18), channel_id=1, source_target_pairs={{0,256},{128,384},{256,0},{384,128},{1,257},{129,385},{257,1},{385... | collective-permute-start | bytes 1376264 | tf_op jit(solution)/shard_map/ppermute | solution.py:423
  27.8 3.1 %collective-permute-start.2 = (f32[16,56,128]{2,1,0:T(8,128)}, f32[16,56,128]{2,1,0:T(8,128)S(1)}, u32[]{:S(2)}, u32[]{:S(2)}) collective-permute-start(f32[16,56,128]{2,1,0:T(8,128)} %get-tuple-element.19), channel_id=1, source_target_pairs={{0,384},{128,0},{256,128},{384,256},{1,385},{129,1},{257,129},{385... | collective-permute-start | bytes 1376264 | tf_op jit(solution)/shard_map/ppermute | solution.py:423
  30.8 3.8 %collective-permute-done.refs_1_ = f32[16,56,128]{2,1,0:T(8,128)S(1)} collective-permute-done((f32[16,56,128]{2,1,0:T(8,128)}, f32[16,56,128]{2,1,0:T(8,128)S(1)}, u32[]{:S(2)}, u32[]{:S(2)}) %collective-permute-start) | collective-permute-done | bytes 458784 | tf_op jit(solution)/shard_map/ppermute | solution.py:423
  34.6 10.8 %collective-permute-done.1.refs_2_ = f32[16,56,128]{2,1,0:T(8,128)S(1)} collective-permute-done((f32[16,56,128]{2,1,0:T(8,128)}, f32[16,56,128]{2,1,0:T(8,128)S(1)}, u32[]{:S(2)}, u32[]{:S(2)}) %collective-permute-start.1) | collective-permute-done | bytes 458784 | tf_op jit(solution)/shard_map/ppermute | solution.py:423
  45.5 2.0 collective-permute-done.2.refs_3_
  47.4 1.0 copy-done.1
  49.3 17.3 %all_to_all.45.blocks_ref = f32[32,8,256]{2,1,0:T(8,128)S(1)} all-to-all(f32[32,8,256]{2,1,0:T(8,128)S(1)} %bitcast.15), channel_id=1, replica_groups=mesh['replica'=4,'fsdp'=16,'tensor'=8] {'replica','tensor'}, dimensions={0} | all-to-all | bytes 524288 | tf_op jit(solution)/shard_map/all_to_all | solution.py:21
  66.7 12.5 %all_to_all.46 = f32[32,8,256]{2,1,0:T(8,128)S(1)} all-to-all(f32[32,8,256]{2,1,0:T(8,128)S(1)} %sum_copies.2), channel_id=1, replica_groups=mesh['replica'=4,'fsdp'=16,'tensor'=8] {'replica','tensor'}, dimensions={0} | all-to-all | bytes 524288 | tf_op jit(solution)/shard_map/all_to_all | solution.py:21
  79.1 1.3 terms.1
  80.4 18.4 %all_to_all.47.blocks_ref = f32[4,256,128]{2,1,0:T(8,128)S(1)} all-to-all(f32[4,256,128]{2,1,0:T(8,128)S(1)} %bitcast.11), channel_id=1, replica_groups={{0,8,16,24},{32,40,48,56},{64,72,80,88},{96,104,112,120},{1,9,17,25},{3..., dimensions={0} | all-to-all | bytes 1048576 | tf_op jit(solution)/shard_map/all_to_all | solution.py:21
  98.8 21.6 %all_to_all.48.blocks_ref = f32[4,64,128]{2,1,0:T(8,128)S(1)} all-to-all(f32[4,64,128]{2,1,0:T(8,128)S(1)} %sum_blocks.1), channel_id=1, replica_groups={{0,32,64,96},{8,40,72,104},{16,48,80,112},{24,56,88,120},{1,33,65,97},{..., dimensions={0} | all-to-all | bytes 262144 | tf_op jit(solution)/shard_map/all_to_all | solution.py:21
  120.4 14.9 %all_to_all.49 = f32[4,64,128]{2,1,0:T(8,128)S(1)} all-to-all(f32[4,64,128]{2,1,0:T(8,128)S(1)} %sum_copies.3), channel_id=1, replica_groups={{0,32,64,96},{8,40,72,104},{16,48,80,112},{24,56,88,120},{1,33,65,97},{..., dimensions={0} | all-to-all | bytes 262144 | tf_op jit(solution)/shard_map/all_to_all | solution.py:21
  135.3 12.4 %all_to_all.50 = f32[4,256,128]{2,1,0:T(8,128)S(1)} all-to-all(f32[4,256,128]{2,1,0:T(8,128)S(1)} %broadcast_in_dim.8), channel_id=1, replica_groups={{0,8,16,24},{32,40,48,56},{64,72,80,88},{96,104,112,120},{1,9,17,25},{3..., dimensions={0} | all-to-all | bytes 1048576 | tf_op jit(solution)/shard_map/all_to_all | solution.py:21
  148.4 10.0 %all-to-all-start.7 = ((f32[8,32,256]{2,1,0:T(8,128)}), f32[8,32,256]{2,1,0:T(8,128)S(1)}, u32[]{:S(2)}, u32[]{:S(2)}) async-start(f32[8,32,256]{2,1,0:T(8,128)} %slab.1), calls=%async_computation.7 | async-start | bytes 524288 | tf_op jit(solution)/shard_map/all_to_all | solution.py:21
  158.4 1.9 collective-permute-start.5
  160.4 3.6 %collective-permute-start.4 = (f32[16,56,128]{2,1,0:T(8,128)S(1)}, f32[16,56,128]{2,1,0:T(8,128)S(1)}, u32[]{:S(2)}, u32[]{:S(2)}) collective-permute-start(f32[16,56,128]{2,1,0:T(8,128)S(1)} %raw.1.raw_ref.refs_0_), channel_id=1, source_target_pairs={{0,256},{128,384},{256,0},{384,128},{1,257},{129,385},{257,1},{385... | collective-permute-start | bytes 1376264 | tf_op jit(solution)/shard_map/ppermute | solution.py:423
  164.0 3.1 %collective-permute-start.3 = (f32[16,56,128]{2,1,0:T(8,128)S(1)}, f32[16,56,128]{2,1,0:T(8,128)S(1)}, u32[]{:S(2)}, u32[]{:S(2)}) collective-permute-start(f32[16,56,128]{2,1,0:T(8,128)S(1)} %raw.1.raw_ref.refs_0_), channel_id=1, source_target_pairs={{0,384},{128,0},{256,128},{384,256},{1,385},{129,1},{257,129},{385... | collective-permute-start | bytes 1376264 | tf_op jit(solution)/shard_map/ppermute | solution.py:423
  167.1 11.2 %factor.1 = (f32[256,256]{1,0:T(8,128)S(1)}, f32[256,256]{1,0:T(8,128)S(1)}, f32[256,256]{1,0:T(8,128)}, f32[32,8,128]{2,1,0:T(8,128)}) custom-call(f32[256,256]{1,0:T(8,128)S(1)} %bitcast.14, f32[256,256]{1,0:T(8,128)S(1)} %bitcast.13, f32[16,56,128]{2,1,0:T(8,128)S(1)} %raw.1.raw_ref.refs_0_), custom_call_target="tpu_custom_call" | custom-call | flops 30000001024 | bytes 1000000 | tf_op jit(solution)/shard_map/factor/pallas_call | solution.py:319
  179.6 7.9 %all-to-all-start.8 = ((f32[32,8,128]{2,1,0:T(8,128)}), f32[32,8,128]{2,1,0:T(8,128)S(1)}, u32[]{:S(2)}, u32[]{:S(2)}) async-start(f32[32,8,128]{2,1,0:T(8,128)} %get-tuple-element.27), calls=%async_computation.8 | async-start | bytes 262144 | tf_op jit(solution)/shard_map/all_to_all | solution.py:21
  189.1 5.9 %update.1 = (f32[1,256,1792]{2,1,0:T(8,128)}, f32[112,256]{1,0:T(8,128)}) custom-call(s32[3]{0:T(128)} %pad_add_fusion.where_ref, f32[1,256,1792]{2,1,0:T(8,128)} %momentum_ref.3, bf16[1,256,1792]{2,1,0:T(8,128)(2,1)} %gradient_ref.3, f32[256,256]{1,0:T(8,128)} %copy-done.3, f32[256,256]{1,0:T(8,128)} %copy-done.2, f32[16,56,128]{2,1,0:T(8,128)} %copy-done, ...), custom_call_target="tpu_custom_call" | custom-call | tf_op jit(solution)/shard_map/update/pallas_call | solution.py:367
  195.2 0.9 copy-done.4
  (31 shorter events, 6.2 us)
Async XLA Ops:
  4.5 42.9 %all-to-all-start = ((f32[16,56,128]{2,1,0:T(8,128)}), f32[16,56,128]{2,1,0:T(8,128)S(1)}, u32[]{:S(2)}, u32[]{:S(2)}) async-start(f32[16,56,128]{2,1,0:T(8,128)} %get-tuple-element.20), calls=%async_computation | async-start | bytes 917504 | tf_op jit(solution)/shard_map/all_to_all | solution.py:21
  20.3 14.4 %collective-permute-start = (f32[16,56,128]{2,1,0:T(8,128)}, f32[16,56,128]{2,1,0:T(8,128)S(1)}, u32[]{:S(2)}, u32[]{:S(2)}) collective-permute-start(f32[16,56,128]{2,1,0:T(8,128)} %get-tuple-element.17), channel_id=1, source_target_pairs={{0,128},{128,256},{256,384},{384,0},{1,129},{129,257},{257,385},{3... | collective-permute-start | bytes 1376264 | tf_op jit(solution)/shard_map/ppermute | solution.py:423
  23.4 22.1 %collective-permute-start.1 = (f32[16,56,128]{2,1,0:T(8,128)}, f32[16,56,128]{2,1,0:T(8,128)S(1)}, u32[]{:S(2)}, u32[]{:S(2)}) collective-permute-start(f32[16,56,128]{2,1,0:T(8,128)} %get-tuple-element.18), channel_id=1, source_target_pairs={{0,256},{128,384},{256,0},{384,128},{1,257},{129,385},{257,1},{385... | collective-permute-start | bytes 1376264 | tf_op jit(solution)/shard_map/ppermute | solution.py:423
  27.8 19.7 %collective-permute-start.2 = (f32[16,56,128]{2,1,0:T(8,128)}, f32[16,56,128]{2,1,0:T(8,128)S(1)}, u32[]{:S(2)}, u32[]{:S(2)}) collective-permute-start(f32[16,56,128]{2,1,0:T(8,128)} %get-tuple-element.19), channel_id=1, source_target_pairs={{0,384},{128,0},{256,128},{384,256},{1,385},{129,1},{257,129},{385... | collective-permute-start | bytes 1376264 | tf_op jit(solution)/shard_map/ppermute | solution.py:423
  47.4 1.0 copy-start.1
  48.5 30.7 %copy-start.5 = (s32[3]{0:T(128)S(1)}, s32[3]{0:T(128)}, u32[]{:S(2)}) copy-start(s32[3]{0:T(128)} %pad_add_fusion.where_ref) | copy-start | bytes 40
  148.4 18.7 %all-to-all-start.7 = ((f32[8,32,256]{2,1,0:T(8,128)}), f32[8,32,256]{2,1,0:T(8,128)S(1)}, u32[]{:S(2)}, u32[]{:S(2)}) async-start(f32[8,32,256]{2,1,0:T(8,128)} %slab.1), calls=%async_computation.7 | async-start | bytes 524288 | tf_op jit(solution)/shard_map/all_to_all | solution.py:21
  158.4 19.8 %copy-start = (f32[16,56,128]{2,1,0:T(8,128)}, f32[16,56,128]{2,1,0:T(8,128)S(1)}, u32[]{:S(2)}) copy-start(f32[16,56,128]{2,1,0:T(8,128)S(1)} %raw.1.raw_ref.refs_0_) | copy-start | bytes 1376260
  158.4 29.1 %collective-permute-start.5 = (f32[16,56,128]{2,1,0:T(8,128)S(1)}, f32[16,56,128]{2,1,0:T(8,128)S(1)}, u32[]{:S(2)}, u32[]{:S(2)}) collective-permute-start(f32[16,56,128]{2,1,0:T(8,128)S(1)} %raw.1.raw_ref.refs_0_), channel_id=1, source_target_pairs={{0,128},{128,256},{256,384},{384,0},{1,129},{129,257},{257,385},{3... | collective-permute-start | bytes 1376264 | tf_op jit(solution)/shard_map/ppermute | solution.py:423
  160.4 27.2 %collective-permute-start.4 = (f32[16,56,128]{2,1,0:T(8,128)S(1)}, f32[16,56,128]{2,1,0:T(8,128)S(1)}, u32[]{:S(2)}, u32[]{:S(2)}) collective-permute-start(f32[16,56,128]{2,1,0:T(8,128)S(1)} %raw.1.raw_ref.refs_0_), channel_id=1, source_target_pairs={{0,256},{128,384},{256,0},{384,128},{1,257},{129,385},{257,1},{385... | collective-permute-start | bytes 1376264 | tf_op jit(solution)/shard_map/ppermute | solution.py:423
  164.0 23.5 %collective-permute-start.3 = (f32[16,56,128]{2,1,0:T(8,128)S(1)}, f32[16,56,128]{2,1,0:T(8,128)S(1)}, u32[]{:S(2)}, u32[]{:S(2)}) collective-permute-start(f32[16,56,128]{2,1,0:T(8,128)S(1)} %raw.1.raw_ref.refs_0_), channel_id=1, source_target_pairs={{0,384},{128,0},{256,128},{384,256},{1,385},{129,1},{257,129},{385... | collective-permute-start | bytes 1376264 | tf_op jit(solution)/shard_map/ppermute | solution.py:423
  178.2 0.7 copy-start.2
  178.9 0.7 copy-start.3
  179.6 15.6 %all-to-all-start.8 = ((f32[32,8,128]{2,1,0:T(8,128)}), f32[32,8,128]{2,1,0:T(8,128)S(1)}, u32[]{:S(2)}, u32[]{:S(2)}) async-start(f32[32,8,128]{2,1,0:T(8,128)} %get-tuple-element.27), calls=%async_computation.8 | async-start | bytes 262144 | tf_op jit(solution)/shard_map/all_to_all | solution.py:21
  187.5 1.6 copy-start.6
  187.5 0.8 copy-start.7
  188.4 0.8 copy-start.8
  195.2 0.9 copy-start.4

commit v3 on v2

--- a/solution.py
+++ b/solution.py
@@ -13,7 +13,7 @@
 PANEL = 64
 NEAR = 4
 LANES = 128
-VMEM_LIMIT = 40 * 1024 * 1024
+VMEM_LIMIT = 20 * 1024 * 1024
 VMEM_WHOLE = 63 * 1024 * 1024
 
 
@@ -42,10 +42,12 @@
     )
 
 
-def turn_kernel(where_ref, momentum_ref, gradient_ref, right_ref, *refs):
-    outs, copies_ref, sorted_rows = refs[:-2], refs[-2], refs[-1]
-    replica = where_ref[0]
-    turned = (momentum_ref[0] + gradient_ref[0].astype(jnp.float32)).T
+def turn_kernel(momentum_ref, gradient_ref, right_ref, *refs):
+    outs, (copies_ref, buffer_ref, sorted_rows) = refs[:-3], refs[-3:]
+    replica = lax.axis_index("replica")
+    buffer = momentum_ref[0] + gradient_ref[0].astype(jnp.float32)
+    buffer_ref[0] = buffer
+    turned = buffer.T
     replicas, blocks, packed = sorted_rows.shape[:3]
     piece = packed // 2
     for block in range(blocks):
@@ -65,7 +67,7 @@
         copies_ref[...] = jnp.broadcast_to(pack(rows)[None], copies_ref.shape)
 
 
-def turn(where, momentum, gradient, right_in, replicas, fsdp_count):
+def turn(momentum, gradient, right_in, replicas, fsdp_count):
     row_count, col_count = momentum.shape[1:]
     own = col_count // fsdp_count
     group = math.lcm(own, LANES)
@@ -73,19 +75,19 @@
     packed = 2 * (own // replicas)
     block = (fsdp_count // steps, packed, LANES)
     whole = (fsdp_count, packed, LANES)
+    columns = pl.BlockSpec((1, row_count, group), lambda i: (0, 0, i))
     return pl.pallas_call(
         turn_kernel,
         grid=(steps,),
-        in_specs=[pl.BlockSpec(memory_space=pltpu.SMEM)]
-        + [pl.BlockSpec((1, row_count, group), lambda i: (0, 0, i))] * 2
-        + [pl.BlockSpec(right_in.shape, lambda i: (0, 0))],
+        in_specs=[columns] * 2 + [pl.BlockSpec(right_in.shape, lambda i: (0, 0))],
         out_specs=[pl.BlockSpec(block, lambda i: (i, 0, 0))] * replicas
-        + [pl.BlockSpec(whole, lambda i: (0, 0, 0))],
-        out_shape=[jax.ShapeDtypeStruct(whole, jnp.float32)] * (replicas + 1),
+        + [pl.BlockSpec(whole, lambda i: (0, 0, 0)), columns],
+        out_shape=[jax.ShapeDtypeStruct(whole, jnp.float32)] * (replicas + 1)
+        + [jax.ShapeDtypeStruct(momentum.shape, jnp.float32)],
         scratch_shapes=[pltpu.VMEM((replicas,) + block, jnp.float32)],
         compiler_params=pltpu.CompilerParams(vmem_limit_bytes=VMEM_WHOLE),
         name="turn",
-    )(where, momentum, gradient, right_in)
+    )(momentum, gradient, right_in)
 
 
 def project_kernel(part_refs, right_ref, sum_ref, out_ref, right):
@@ -153,14 +155,14 @@
     )(blocks)
 
 
-def terms_kernel(share, where_ref, sum_ref, projected_ref, out_ref, gram):
+def terms_kernel(share, sum_ref, projected_ref, out_ref, gram):
     near, far, packed = out_ref.shape[:3]
     blocks = near * far
     piece = sum_ref.shape[0] // blocks
     slab = share * blocks
     projected = projected_ref[...]
     gram[...] = column_dot(projected, projected)
-    rows = gram[pl.ds(pl.multiple_of(where_ref[2] * slab, slab), slab), :]
+    rows = gram[pl.ds(pl.multiple_of(lax.axis_index("tensor") * slab, slab), slab), :]
     raw = jnp.dot(
         sum_ref[...], projected, precision=HIGHEST, preferred_element_type=jnp.float32
     )
@@ -172,20 +174,17 @@
         out_ref[b, a, 2 * piece :, :] = jnp.concatenate([tail, rest], axis=0)
 
 
-def make_terms(where, column_sum, projected, blocks, tensor_count):
+def make_terms(column_sum, projected, blocks, tensor_count):
     rank = projected.shape[1]
     share = rank // tensor_count // blocks
     packed = 2 * (column_sum.shape[0] // blocks + share)
-    whole = pl.BlockSpec(memory_space=pltpu.VMEM)
     return pl.pallas_call(
         functools.partial(terms_kernel, share),
-        in_specs=[pl.BlockSpec(memory_space=pltpu.SMEM), whole, whole],
-        out_specs=whole,
         out_shape=jax.ShapeDtypeStruct((NEAR, blocks // NEAR, -(-packed // 8) * 8, LANES), jnp.float32),
         scratch_shapes=[pltpu.VMEM((rank, rank), jnp.float32)],
         compiler_params=pltpu.CompilerParams(vmem_limit_bytes=VMEM_LIMIT),
         name="terms",
-    )(where, column_sum, projected)
+    )(column_sum, projected)
 
 
 def slab_kernel(packed, sums_ref, slab_ref):
@@ -334,28 +333,29 @@
     )(gram_matrix, projected, raw_quarter)
 
 
-def update_kernel(where_ref, momentum_ref, gradient_ref, ortho_ref, inverse_ref, *refs):
+def update_kernel(buffer_ref, ortho_ref, inverse_ref, *refs):
     parts, (out_ref, own_ref, sorted_rows, raw) = refs[:-4], refs[-4:]
     replicas, blocks, packed = sorted_rows.shape[:3]
     piece = packed // 2
     own = replicas * piece
+    place, own_block = lax.axis_index("replica"), lax.axis_index("fsdp")
     for step, part_ref in enumerate(parts):
-        sorted_rows[lax.rem(where_ref[0] + step, replicas)] = part_ref[...]
+        sorted_rows[lax.rem(place + step, replicas)] = part_ref[...]
     for block in range(blocks):
         for replica in range(replicas):
             start = block * own + replica * piece
             raw[start : start + piece, :] = unpack(sorted_rows[replica, block])
     correction = row_dot(ortho_ref[...], raw[...])
-    out_ref[0] = momentum_ref[0] + gradient_ref[0].astype(jnp.float32) - 0.1 * correction
-
-    @pl.when(where_ref[1] // blocks == pl.program_id(0))
+    out_ref[0] = buffer_ref[0] - 0.1 * correction
+
+    @pl.when(own_block // blocks == pl.program_id(0))
     def _():
-        start = pl.multiple_of(lax.rem(where_ref[1], blocks) * own, 8)
+        start = pl.multiple_of(lax.rem(own_block, blocks) * own, 8)
         own_ref[...] = row_dot(raw[pl.ds(start, own), :], inverse_ref[...])
 
 
-def update(where, momentum, gradient, orthonormal, inverse, parts):
-    row_count, own_count = momentum.shape[1:]
+def update(buffer, orthonormal, inverse, parts):
+    row_count, own_count = buffer.shape[1:]
     replicas = len(parts)
     fsdp_count, packed, _ = parts[0].shape
     rank = orthonormal.shape[1]
@@ -368,8 +368,6 @@
         update_kernel,
         grid=(steps,),
         in_specs=[
-            pl.BlockSpec(memory_space=pltpu.SMEM),
-            columns,
             columns,
             pl.BlockSpec((row_count, rank), lambda i: (0, 0)),
             pl.BlockSpec((rank, rank), lambda i: (0, 0)),
@@ -377,16 +375,17 @@
         + [pl.BlockSpec(block, lambda i: (i, 0, 0))] * replicas,
         out_specs=[columns, pl.BlockSpec((own, rank), lambda i: (0, 0))],
         out_shape=[
-            jax.ShapeDtypeStruct(momentum.shape, jnp.float32),
+            jax.ShapeDtypeStruct(buffer.shape, jnp.float32),
             jax.ShapeDtypeStruct((own, rank), jnp.float32),
         ],
         scratch_shapes=[
             pltpu.VMEM((replicas,) + block, jnp.float32),
             pltpu.VMEM((group, rank), jnp.float32),
         ],
-        compiler_params=pltpu.CompilerParams(vmem_limit_bytes=VMEM_WHOLE),
+        compiler_params=pltpu.CompilerParams(vmem_limit_bytes=VMEM_LIMIT),
+        input_output_aliases={0: 0},
         name="update",
-    )(where, momentum, gradient, orthonormal, inverse, *parts)
+    )(buffer, orthonormal, inverse, *parts)
 
 
 def scale_kernel(columns, own_ref, squares_ref, out_ref):
@@ -410,7 +409,6 @@
     fsdp_count = lax.axis_size("fsdp")
     tensor_count = lax.axis_size("tensor")
     group_count = replicas * tensor_count
-    where = jnp.stack([lax.axis_index("replica"), lax.axis_index("fsdp"), lax.axis_index("tensor")])
     band = row_count // group_count
     packed = 2 * (col_count // fsdp_count // replicas)
     slab = rank // tensor_count
@@ -422,7 +420,7 @@
         pairs = [(i, (i + step) % replicas) for i in range(replicas)]
         return lax.ppermute(value, "replica", pairs)
 
-    *turned, right_copies = turn(where, momentum, gradient, right_in, replicas, fsdp_count)
+    *turned, right_copies, buffer = turn(momentum, gradient, right_in, replicas, fsdp_count)
     right_quarter = exchange(right_copies, "fsdp")
     parts = [turned[0]] + [around(turned[step], step) for step in range(1, replicas)]
     column_sum, partial_value = project(parts, right_quarter)
@@ -430,7 +428,7 @@
     partial_value = exchange(partial_value.reshape(group_count, band, rank), GROUP)
     projected = exchange(sum_copies(partial_value, 1.0 / replicas), GROUP).reshape(row_count, rank)
 
-    terms = make_terms(where, column_sum, projected, fsdp_count, tensor_count)
+    terms = make_terms(column_sum, projected, fsdp_count, tensor_count)
     height = terms.shape[2]
     terms = exchange(terms.reshape(NEAR, far * height, LANES), "fsdp", near_groups)
     sums = exchange(sum_blocks(terms, far), "fsdp", far_groups)
@@ -443,7 +441,7 @@
     inverse, combined, left_factor, squares = make_factor(
         gram_matrix, projected, raw_quarter, replicas, row_count * fsdp_count, group_count
     )
-    new_momentum, own_rows = update(where, momentum, gradient, combined, inverse, raw_parts)
+    new_momentum, own_rows = update(buffer, combined, inverse, raw_parts)
     right_factor = make_right(own_rows, exchange(squares, GROUP), col_count * tensor_count)
     return (left_factor, right_factor, new_momentum)
 

time: 198 us -> 195 us (0.985)
  local copies, waits for them, and re-layouts: 4.95 us -> 1.05 us
  waiting for transfers between devices: 16.8 us -> 19.3 us
    unnamed x18 -> x2, local copies, waits for them, and re-layouts: 4.92 us -> 1.02 us
    all_to_all x3, waiting for transfers between devices: 0.2 us -> 2.7 us  [exchange(): lax.all_to_all(blocks, axes, 0, 0, tiled=True, axis_index_groups=groups)]
  transfers between devices with their start and end apart: 9 -> 9, of which waited for: 4 -> 4; matrix products, arithmetic and copies ran while one was open for 0% -> 0% of each run, Pallas kernels for 9% -> 8%
where the time goes in v3:
time: 195 us; the launch traced here: 194 us
  blocking collectives  97 us (50%)
  starting transfers between devices  52.7 us (27%)
  Pallas kernels  23 us (12%)
  waiting for transfers between devices  19.3 us (10%)
    all_to_all x6, blocking collectives, exchange(): lax.all_to_all(blocks, axes, 0, 0, tiled=True, axis_index_groups=groups)  97 us
    all_to_all x3, starting transfers between devices, exchange(): lax.all_to_all(blocks, axes, 0, 0, tiled=True, axis_index_groups=groups)  33.6 us
    ppermute x6, starting transfers between devices, around(): return lax.ppermute(value, 'replica', pairs)  19.2 us
    ppermute x6, waiting for transfers between devices, around(): return lax.ppermute(value, 'replica', pairs)  16.6 us
    pallas_call x1, Pallas kernels, make_factor(): pl.pallas_call(functools.partial(factor_kernel, replicas, rows), out_shap...  11.2 us
    pallas_call x1, Pallas kernels, update(): pl.pallas_call(update_kernel, grid=(steps,), in_specs=[columns, pl.BlockS...  4.97 us
  transfers between devices with their start and end apart: 9, of which 4 were waited for; matrix products, arithmetic and copies ran while one was open for 0% of the time, Pallas kernels for 8%

profile of v3, /device:TPU:1, one launch (start us, length us, event | category | flops | bytes accessed | tf_op | source)
XLA Modules:
  0.0 193.8 jit_solution(2505615562966671843)
XLA Ops:
  0.6 3.7 %turn.1 = (f32[16,56,128]{2,1,0:T(8,128)}, f32[16,56,128]{2,1,0:T(8,128)}, f32[16,56,128]{2,1,0:T(8,128)}, f32[16,56,128]{2,1,0:T(8,128)}, f32[16,56,128]{2,1,0:T(8,128)}, /*index=5*/f32[1,256,1792]{2,1,0:T(8,128)}) custom-call(f32[1,256,1792]{2,1,0:T(8,128)} %momentum_ref.1, bf16[1,256,1792]{2,1,0:T(8,128)(2,1)} %gradient_ref.1, f32[112,256]{1,0:T(8,128)} %right_ref.1), custom_call_target="tpu_custom_call" | custom-call | tf_op jit(solution)/shard_map/turn/pallas_call | solution.py:79
  4.4 15.7 %all-to-all-start = ((f32[16,56,128]{2,1,0:T(8,128)}), f32[16,56,128]{2,1,0:T(8,128)S(1)}, u32[]{:S(2)}, u32[]{:S(2)}) async-start(f32[16,56,128]{2,1,0:T(8,128)} %get-tuple-element.21), calls=%async_computation | async-start | bytes 917504 | tf_op jit(solution)/shard_map/all_to_all | solution.py:21
  20.1 3.1 %collective-permute-start = (f32[16,56,128]{2,1,0:T(8,128)}, f32[16,56,128]{2,1,0:T(8,128)S(1)}, u32[]{:S(2)}, u32[]{:S(2)}) collective-permute-start(f32[16,56,128]{2,1,0:T(8,128)} %get-tuple-element.18), channel_id=1, source_target_pairs={{0,128},{128,256},{256,384},{384,0},{1,129},{129,257},{257,385},{3... | collective-permute-start | bytes 1376264 | tf_op jit(solution)/shard_map/ppermute | solution.py:421
  23.3 4.4 %collective-permute-start.1 = (f32[16,56,128]{2,1,0:T(8,128)}, f32[16,56,128]{2,1,0:T(8,128)S(1)}, u32[]{:S(2)}, u32[]{:S(2)}) collective-permute-start(f32[16,56,128]{2,1,0:T(8,128)} %get-tuple-element.19), channel_id=1, source_target_pairs={{0,256},{128,384},{256,0},{384,128},{1,257},{129,385},{257,1},{385... | collective-permute-start | bytes 1376264 | tf_op jit(solution)/shard_map/ppermute | solution.py:421
  27.6 3.1 %collective-permute-start.2 = (f32[16,56,128]{2,1,0:T(8,128)}, f32[16,56,128]{2,1,0:T(8,128)S(1)}, u32[]{:S(2)}, u32[]{:S(2)}) collective-permute-start(f32[16,56,128]{2,1,0:T(8,128)} %get-tuple-element.20), channel_id=1, source_target_pairs={{0,384},{128,0},{256,128},{384,256},{1,385},{129,1},{257,129},{385... | collective-permute-start | bytes 1376264 | tf_op jit(solution)/shard_map/ppermute | solution.py:421
  30.7 3.8 %collective-permute-done.refs_1_ = f32[16,56,128]{2,1,0:T(8,128)S(1)} collective-permute-done((f32[16,56,128]{2,1,0:T(8,128)}, f32[16,56,128]{2,1,0:T(8,128)S(1)}, u32[]{:S(2)}, u32[]{:S(2)}) %collective-permute-start) | collective-permute-done | bytes 458784 | tf_op jit(solution)/shard_map/ppermute | solution.py:421
  34.5 10.8 %collective-permute-done.1.refs_2_ = f32[16,56,128]{2,1,0:T(8,128)S(1)} collective-permute-done((f32[16,56,128]{2,1,0:T(8,128)}, f32[16,56,128]{2,1,0:T(8,128)S(1)}, u32[]{:S(2)}, u32[]{:S(2)}) %collective-permute-start.1) | collective-permute-done | bytes 458784 | tf_op jit(solution)/shard_map/ppermute | solution.py:421
  45.3 2.0 %collective-permute-done.2.refs_3_ = f32[16,56,128]{2,1,0:T(8,128)S(1)} collective-permute-done((f32[16,56,128]{2,1,0:T(8,128)}, f32[16,56,128]{2,1,0:T(8,128)S(1)}, u32[]{:S(2)}, u32[]{:S(2)}) %collective-permute-start.2) | collective-permute-done | bytes 458784 | tf_op jit(solution)/shard_map/ppermute | solution.py:421
  47.3 1.0 copy-done
  48.3 0.8 project.1
  49.1 17.3 %all_to_all.45.blocks_ref = f32[32,8,256]{2,1,0:T(8,128)S(1)} all-to-all(f32[32,8,256]{2,1,0:T(8,128)S(1)} %bitcast.12), channel_id=1, replica_groups=mesh['replica'=4,'fsdp'=16,'tensor'=8] {'replica','tensor'}, dimensions={0} | all-to-all | bytes 524288 | tf_op jit(solution)/shard_map/all_to_all | solution.py:21
  66.5 12.5 %all_to_all.46 = f32[32,8,256]{2,1,0:T(8,128)S(1)} all-to-all(f32[32,8,256]{2,1,0:T(8,128)S(1)} %sum_copies.2), channel_id=1, replica_groups=mesh['replica'=4,'fsdp'=16,'tensor'=8] {'replica','tensor'}, dimensions={0} | all-to-all | bytes 524288 | tf_op jit(solution)/shard_map/all_to_all | solution.py:21
  79.7 18.4 %all_to_all.47.blocks_ref = f32[4,256,128]{2,1,0:T(8,128)S(1)} all-to-all(f32[4,256,128]{2,1,0:T(8,128)S(1)} %bitcast.8), channel_id=1, replica_groups={{0,8,16,24},{32,40,48,56},{64,72,80,88},{96,104,112,120},{1,9,17,25},{3..., dimensions={0} | all-to-all | bytes 1048576 | tf_op jit(solution)/shard_map/all_to_all | solution.py:21
  98.1 21.6 %all_to_all.48.blocks_ref = f32[4,64,128]{2,1,0:T(8,128)S(1)} all-to-all(f32[4,64,128]{2,1,0:T(8,128)S(1)} %sum_blocks.1), channel_id=1, replica_groups={{0,32,64,96},{8,40,72,104},{16,48,80,112},{24,56,88,120},{1,33,65,97},{..., dimensions={0} | all-to-all | bytes 262144 | tf_op jit(solution)/shard_map/all_to_all | solution.py:21
  119.7 14.9 %all_to_all.49 = f32[4,64,128]{2,1,0:T(8,128)S(1)} all-to-all(f32[4,64,128]{2,1,0:T(8,128)S(1)} %sum_copies.3), channel_id=1, replica_groups={{0,32,64,96},{8,40,72,104},{16,48,80,112},{24,56,88,120},{1,33,65,97},{..., dimensions={0} | all-to-all | bytes 262144 | tf_op jit(solution)/shard_map/all_to_all | solution.py:21
  134.6 12.4 %all_to_all.50 = f32[4,256,128]{2,1,0:T(8,128)S(1)} all-to-all(f32[4,256,128]{2,1,0:T(8,128)S(1)} %broadcast_in_dim.8), channel_id=1, replica_groups={{0,8,16,24},{32,40,48,56},{64,72,80,88},{96,104,112,120},{1,9,17,25},{3..., dimensions={0} | all-to-all | bytes 1048576 | tf_op jit(solution)/shard_map/all_to_all | solution.py:21
  147.7 10.0 %all-to-all-start.7 = ((f32[8,32,256]{2,1,0:T(8,128)}), f32[8,32,256]{2,1,0:T(8,128)S(1)}, u32[]{:S(2)}, u32[]{:S(2)}) async-start(f32[8,32,256]{2,1,0:T(8,128)} %slab.1), calls=%async_computation.7 | async-start | bytes 524288 | tf_op jit(solution)/shard_map/all_to_all | solution.py:21
  157.7 1.9 collective-permute-start.5
  159.7 3.6 %collective-permute-start.4 = (f32[16,56,128]{2,1,0:T(8,128)S(1)}, f32[16,56,128]{2,1,0:T(8,128)S(1)}, u32[]{:S(2)}, u32[]{:S(2)}) collective-permute-start(f32[16,56,128]{2,1,0:T(8,128)S(1)} %raw.1.raw_ref.refs_0_), channel_id=1, source_target_pairs={{0,256},{128,384},{256,0},{384,128},{1,257},{129,385},{257,1},{385... | collective-permute-start | bytes 1376264 | tf_op jit(solution)/shard_map/ppermute | solution.py:421
  163.3 3.1 %collective-permute-start.3 = (f32[16,56,128]{2,1,0:T(8,128)S(1)}, f32[16,56,128]{2,1,0:T(8,128)S(1)}, u32[]{:S(2)}, u32[]{:S(2)}) collective-permute-start(f32[16,56,128]{2,1,0:T(8,128)S(1)} %raw.1.raw_ref.refs_0_), channel_id=1, source_target_pairs={{0,384},{128,0},{256,128},{384,256},{1,385},{129,1},{257,129},{385... | collective-permute-start | bytes 1376264 | tf_op jit(solution)/shard_map/ppermute | solution.py:421
  166.4 11.2 %factor.1 = (f32[256,256]{1,0:T(8,128)S(1)}, f32[256,256]{1,0:T(8,128)S(1)}, f32[256,256]{1,0:T(8,128)}, f32[32,8,128]{2,1,0:T(8,128)}) custom-call(f32[256,256]{1,0:T(8,128)S(1)} %bitcast.11, f32[256,256]{1,0:T(8,128)S(1)} %bitcast.10, f32[16,56,128]{2,1,0:T(8,128)S(1)} %raw.1.raw_ref.refs_0_), custom_call_target="tpu_custom_call" | custom-call | flops 30000001024 | bytes 1000000 | tf_op jit(solution)/shard_map/factor/pallas_call | solution.py:318
  177.5 7.9 %all-to-all-start.8 = ((f32[32,8,128]{2,1,0:T(8,128)}), f32[32,8,128]{2,1,0:T(8,128)S(1)}, u32[]{:S(2)}, u32[]{:S(2)}) async-start(f32[32,8,128]{2,1,0:T(8,128)} %get-tuple-element.29), calls=%async_computation.8 | async-start | bytes 262144 | tf_op jit(solution)/shard_map/all_to_all | solution.py:21
  185.4 5.0 %update.1 = (f32[1,256,1792]{2,1,0:T(8,128)}, f32[112,256]{1,0:T(8,128)S(1)}) custom-call(f32[1,256,1792]{2,1,0:T(8,128)} %get-tuple-element.25.buffer_ref, f32[256,256]{1,0:T(8,128)S(1)} %get-tuple-element.26.ortho_ref, f32[256,256]{1,0:T(8,128)S(1)} %get-tuple-element.27.inverse_ref, ...), custom_call_target="tpu_custom_call", output_to_operand_aliasing={{0}: (0, {})} | custom-call | tf_op jit(solution)/shard_map/update/pallas_call | solution.py:367
  190.4 2.7 %all-to-all-done.8.squares_ref = f32[32,8,128]{2,1,0:T(8,128)S(1)} async-done(((f32[32,8,128]{2,1,0:T(8,128)}), f32[32,8,128]{2,1,0:T(8,128)S(1)}, u32[]{:S(2)}, u32[]{:S(2)}) %all-to-all-start.8) | async-done | bytes 131104 | tf_op jit(solution)/shard_map/all_to_all | solution.py:21
  (14 shorter events, 2.4 us)
Async XLA Ops:
  4.4 42.9 %all-to-all-start = ((f32[16,56,128]{2,1,0:T(8,128)}), f32[16,56,128]{2,1,0:T(8,128)S(1)}, u32[]{:S(2)}, u32[]{:S(2)}) async-start(f32[16,56,128]{2,1,0:T(8,128)} %get-tuple-element.21), calls=%async_computation | async-start | bytes 917504 | tf_op jit(solution)/shard_map/all_to_all | solution.py:21
  20.1 14.4 %collective-permute-start = (f32[16,56,128]{2,1,0:T(8,128)}, f32[16,56,128]{2,1,0:T(8,128)S(1)}, u32[]{:S(2)}, u32[]{:S(2)}) collective-permute-start(f32[16,56,128]{2,1,0:T(8,128)} %get-tuple-element.18), channel_id=1, source_target_pairs={{0,128},{128,256},{256,384},{384,0},{1,129},{129,257},{257,385},{3... | collective-permute-start | bytes 1376264 | tf_op jit(solution)/shard_map/ppermute | solution.py:421
  23.3 22.1 %collective-permute-start.1 = (f32[16,56,128]{2,1,0:T(8,128)}, f32[16,56,128]{2,1,0:T(8,128)S(1)}, u32[]{:S(2)}, u32[]{:S(2)}) collective-permute-start(f32[16,56,128]{2,1,0:T(8,128)} %get-tuple-element.19), channel_id=1, source_target_pairs={{0,256},{128,384},{256,0},{384,128},{1,257},{129,385},{257,1},{385... | collective-permute-start | bytes 1376264 | tf_op jit(solution)/shard_map/ppermute | solution.py:421
  27.6 19.7 %collective-permute-start.2 = (f32[16,56,128]{2,1,0:T(8,128)}, f32[16,56,128]{2,1,0:T(8,128)S(1)}, u32[]{:S(2)}, u32[]{:S(2)}) collective-permute-start(f32[16,56,128]{2,1,0:T(8,128)} %get-tuple-element.20), channel_id=1, source_target_pairs={{0,384},{128,0},{256,128},{384,256},{1,385},{129,1},{257,129},{385... | collective-permute-start | bytes 1376264 | tf_op jit(solution)/shard_map/ppermute | solution.py:421
  47.3 1.0 copy-start
  147.7 18.7 %all-to-all-start.7 = ((f32[8,32,256]{2,1,0:T(8,128)}), f32[8,32,256]{2,1,0:T(8,128)S(1)}, u32[]{:S(2)}, u32[]{:S(2)}) async-start(f32[8,32,256]{2,1,0:T(8,128)} %slab.1), calls=%async_computation.7 | async-start | bytes 524288 | tf_op jit(solution)/shard_map/all_to_all | solution.py:21
  157.7 27.7 %collective-permute-start.5 = (f32[16,56,128]{2,1,0:T(8,128)S(1)}, f32[16,56,128]{2,1,0:T(8,128)S(1)}, u32[]{:S(2)}, u32[]{:S(2)}) collective-permute-start(f32[16,56,128]{2,1,0:T(8,128)S(1)} %raw.1.raw_ref.refs_0_), channel_id=1, source_target_pairs={{0,128},{128,256},{256,384},{384,0},{1,129},{129,257},{257,385},{3... | collective-permute-start | bytes 1376264 | tf_op jit(solution)/shard_map/ppermute | solution.py:421
  159.7 25.8 %collective-permute-start.4 = (f32[16,56,128]{2,1,0:T(8,128)S(1)}, f32[16,56,128]{2,1,0:T(8,128)S(1)}, u32[]{:S(2)}, u32[]{:S(2)}) collective-permute-start(f32[16,56,128]{2,1,0:T(8,128)S(1)} %raw.1.raw_ref.refs_0_), channel_id=1, source_target_pairs={{0,256},{128,384},{256,0},{384,128},{1,257},{129,385},{257,1},{385... | collective-permute-start | bytes 1376264 | tf_op jit(solution)/shard_map/ppermute | solution.py:421
  163.3 22.1 %collective-permute-start.3 = (f32[16,56,128]{2,1,0:T(8,128)S(1)}, f32[16,56,128]{2,1,0:T(8,128)S(1)}, u32[]{:S(2)}, u32[]{:S(2)}) collective-permute-start(f32[16,56,128]{2,1,0:T(8,128)S(1)} %raw.1.raw_ref.refs_0_), channel_id=1, source_target_pairs={{0,384},{128,0},{256,128},{384,256},{1,385},{129,1},{257,129},{385... | collective-permute-start | bytes 1376264 | tf_op jit(solution)/shard_map/ppermute | solution.py:421
  177.5 15.6 %all-to-all-start.8 = ((f32[32,8,128]{2,1,0:T(8,128)}), f32[32,8,128]{2,1,0:T(8,128)S(1)}, u32[]{:S(2)}, u32[]{:S(2)}) async-start(f32[32,8,128]{2,1,0:T(8,128)} %get-tuple-element.29), calls=%async_computation.8 | async-start | bytes 262144 | tf_op jit(solution)/shard_map/all_to_all | solution.py:21

commit v4 on v3

--- a/solution.py
+++ b/solution.py
@@ -289,22 +289,14 @@
             work[below:, :] = rest - column_dot((whole * scale)[:, first:], unit)[below - first :]
 
 
-def factor_kernel(
-    replicas, rows, gram_ref, projected_ref, raw_ref, inverse_ref, ortho_ref, left_ref, squares_ref, work, raw
-):
+def factor_kernel(replicas, gram_ref, raw_ref, inverse_ref, squares_ref, work, raw):
     blocks, packed = raw_ref.shape[:2]
     piece = packed // 2
     for block in range(blocks):
         raw[block * piece : (block + 1) * piece, :] = unpack(raw_ref[block])
     work[...] = gram_ref[...]
     invert_factor(work, inverse_ref)
-    inverse = inverse_ref[...]
-    ortho = row_dot(projected_ref[...], inverse)
-    ortho_ref[...] = jnp.dot(
-        ortho, inverse, precision=HIGHEST, preferred_element_type=jnp.float32
-    ) * (1.0 / replicas)
-    left_ref[...] = ortho * math.sqrt(rows)
-    inverse = inverse * (1.0 / replicas)
+    inverse = inverse_ref[...] * (1.0 / replicas)
     inverse_ref[...] = inverse
     back = row_dot(raw[...], inverse)
     squares = pack(jnp.sum(back * back, axis=0, keepdims=True))
@@ -312,15 +304,13 @@
     squares_ref[...] = jnp.broadcast_to(jnp.concatenate([squares, rest], axis=0)[None], squares_ref.shape)
 
 
-def make_factor(gram_matrix, projected, raw_quarter, replicas, rows, group_count):
+def make_factor(gram_matrix, raw_quarter, replicas, group_count):
     rank = gram_matrix.shape[0]
     blocks, packed, _ = raw_quarter.shape
     return pl.pallas_call(
-        functools.partial(factor_kernel, replicas, rows),
+        functools.partial(factor_kernel, replicas),
         out_shape=[
             jax.ShapeDtypeStruct(gram_matrix.shape, jnp.float32),
-            jax.ShapeDtypeStruct(projected.shape, jnp.float32),
-            jax.ShapeDtypeStruct(projected.shape, jnp.float32),
             jax.ShapeDtypeStruct((group_count, 8, LANES), jnp.float32),
         ],
         scratch_shapes=[
@@ -330,7 +320,25 @@
         compiler_params=pltpu.CompilerParams(vmem_limit_bytes=VMEM_LIMIT),
         cost_estimate=pl.CostEstimate(flops=3 * 10**10, bytes_accessed=10**6, transcendentals=0),
         name="factor",
-    )(gram_matrix, projected, raw_quarter)
+    )(gram_matrix, raw_quarter)
+
+
+def combine_kernel(replicas, rows, projected_ref, inverse_ref, left_ref, combined_ref):
+    inverse = inverse_ref[...]
+    ortho = row_dot(projected_ref[...], inverse) * replicas
+    left_ref[...] = ortho * math.sqrt(rows)
+    combined_ref[...] = jnp.dot(
+        ortho, inverse, precision=HIGHEST, preferred_element_type=jnp.float32
+    )
+
+
+def combine(projected, inverse, replicas, rows):
+    return pl.pallas_call(
+        functools.partial(combine_kernel, replicas, rows),
+        out_shape=[jax.ShapeDtypeStruct(projected.shape, jnp.float32)] * 2,
+        compiler_params=pltpu.CompilerParams(vmem_limit_bytes=VMEM_LIMIT),
+        name="combine",
+    )(projected, inverse)
 
 
 def update_kernel(buffer_ref, ortho_ref, inverse_ref, *refs):
@@ -438,9 +446,8 @@
     gram_matrix = exchange(take_slab(sums, packed, slab, tensor_count), "tensor").reshape(rank, rank)
     raw_quarter = take_raw(sums, packed)
     raw_parts = [raw_quarter] + [around(raw_quarter, -step) for step in range(1, replicas)]
-    inverse, combined, left_factor, squares = make_factor(
-        gram_matrix, projected, raw_quarter, replicas, row_count * fsdp_count, group_count
-    )
+    inverse, squares = make_factor(gram_matrix, raw_quarter, replicas, group_count)
+    left_factor, combined = combine(projected, inverse, replicas, row_count * fsdp_count)
     new_momentum, own_rows = update(buffer, combined, inverse, raw_parts)
     right_factor = make_right(own_rows, exchange(squares, GROUP), col_count * tensor_count)
     return (left_factor, right_factor, new_momentum)

time: 195 us -> 194 us (level)
    pallas_call x1 -> x2, Pallas kernels: 11.2 us -> 11.7 us  [the longest x1 10.4 us: make_factor(): pl.pallas_call(functools.partial(factor_kernel, replicas), out_shape=[jax...]
  transfers between devices with their start and end apart: 9 -> 9, of which waited for: 4 -> 4; matrix products, arithmetic and copies ran while one was open for 0% -> 0% of each run, Pallas kernels for 8% -> 9%
where the time goes in v4:
time: 194 us; the launch traced here: 193 us
  blocking collectives  97 us (50%)
  starting transfers between devices  52.7 us (27%)
  Pallas kernels  23.5 us (12%)
  waiting for transfers between devices  18 us (9%)
    all_to_all x6, blocking collectives, exchange(): lax.all_to_all(blocks, axes, 0, 0, tiled=True, axis_index_groups=groups)  97 us
    all_to_all x3, starting transfers between devices, exchange(): lax.all_to_all(blocks, axes, 0, 0, tiled=True, axis_index_groups=groups)  33.6 us
    ppermute x6, starting transfers between devices, around(): return lax.ppermute(value, 'replica', pairs)  19.2 us
    ppermute x6, waiting for transfers between devices, around(): return lax.ppermute(value, 'replica', pairs)  16.6 us
    pallas_call x1, Pallas kernels, make_factor(): pl.pallas_call(functools.partial(factor_kernel, replicas), out_shape=[jax...  10.4 us
    pallas_call x1, Pallas kernels, update(): pl.pallas_call(update_kernel, grid=(steps,), in_specs=[columns, pl.BlockS...  4.97 us
  transfers between devices with their start and end apart: 9, of which 4 were waited for; matrix products, arithmetic and copies ran while one was open for 0% of the time, Pallas kernels for 9%

profile of v4, /device:TPU:1, one launch (start us, length us, event | category | flops | bytes accessed | tf_op | source)
XLA Modules:
  0.0 193.0 jit_solution(10894007957952042722)
XLA Ops:
  0.6 3.7 %turn.1 = (f32[16,56,128]{2,1,0:T(8,128)}, f32[16,56,128]{2,1,0:T(8,128)}, f32[16,56,128]{2,1,0:T(8,128)}, f32[16,56,128]{2,1,0:T(8,128)}, f32[16,56,128]{2,1,0:T(8,128)}, /*index=5*/f32[1,256,1792]{2,1,0:T(8,128)}) custom-call(f32[1,256,1792]{2,1,0:T(8,128)} %momentum_ref.1, bf16[1,256,1792]{2,1,0:T(8,128)(2,1)} %gradient_ref.1, f32[112,256]{1,0:T(8,128)} %right_ref.1), custom_call_target="tpu_custom_call" | custom-call | tf_op jit(solution)/shard_map/turn/pallas_call | solution.py:79
  4.4 15.7 %all-to-all-start = ((f32[16,56,128]{2,1,0:T(8,128)}), f32[16,56,128]{2,1,0:T(8,128)S(1)}, u32[]{:S(2)}, u32[]{:S(2)}) async-start(f32[16,56,128]{2,1,0:T(8,128)} %get-tuple-element.21), calls=%async_computation | async-start | bytes 917504 | tf_op jit(solution)/shard_map/all_to_all | solution.py:21
  20.1 3.1 %collective-permute-start = (f32[16,56,128]{2,1,0:T(8,128)}, f32[16,56,128]{2,1,0:T(8,128)S(1)}, u32[]{:S(2)}, u32[]{:S(2)}) collective-permute-start(f32[16,56,128]{2,1,0:T(8,128)} %get-tuple-element.18), channel_id=1, source_target_pairs={{0,128},{128,256},{256,384},{384,0},{1,129},{129,257},{257,385},{3... | collective-permute-start | bytes 1376264 | tf_op jit(solution)/shard_map/ppermute | solution.py:429
  23.3 4.4 %collective-permute-start.1 = (f32[16,56,128]{2,1,0:T(8,128)}, f32[16,56,128]{2,1,0:T(8,128)S(1)}, u32[]{:S(2)}, u32[]{:S(2)}) collective-permute-start(f32[16,56,128]{2,1,0:T(8,128)} %get-tuple-element.19), channel_id=1, source_target_pairs={{0,256},{128,384},{256,0},{384,128},{1,257},{129,385},{257,1},{385... | collective-permute-start | bytes 1376264 | tf_op jit(solution)/shard_map/ppermute | solution.py:429
  27.6 3.1 %collective-permute-start.2 = (f32[16,56,128]{2,1,0:T(8,128)}, f32[16,56,128]{2,1,0:T(8,128)S(1)}, u32[]{:S(2)}, u32[]{:S(2)}) collective-permute-start(f32[16,56,128]{2,1,0:T(8,128)} %get-tuple-element.20), channel_id=1, source_target_pairs={{0,384},{128,0},{256,128},{384,256},{1,385},{129,1},{257,129},{385... | collective-permute-start | bytes 1376264 | tf_op jit(solution)/shard_map/ppermute | solution.py:429
  30.7 3.8 %collective-permute-done.refs_1_ = f32[16,56,128]{2,1,0:T(8,128)S(1)} collective-permute-done((f32[16,56,128]{2,1,0:T(8,128)}, f32[16,56,128]{2,1,0:T(8,128)S(1)}, u32[]{:S(2)}, u32[]{:S(2)}) %collective-permute-start) | collective-permute-done | bytes 458784 | tf_op jit(solution)/shard_map/ppermute | solution.py:429
  34.5 10.8 %collective-permute-done.1.refs_2_ = f32[16,56,128]{2,1,0:T(8,128)S(1)} collective-permute-done((f32[16,56,128]{2,1,0:T(8,128)}, f32[16,56,128]{2,1,0:T(8,128)S(1)}, u32[]{:S(2)}, u32[]{:S(2)}) %collective-permute-start.1) | collective-permute-done | bytes 458784 | tf_op jit(solution)/shard_map/ppermute | solution.py:429
  45.3 2.0 %collective-permute-done.2.refs_3_ = f32[16,56,128]{2,1,0:T(8,128)S(1)} collective-permute-done((f32[16,56,128]{2,1,0:T(8,128)}, f32[16,56,128]{2,1,0:T(8,128)S(1)}, u32[]{:S(2)}, u32[]{:S(2)}) %collective-permute-start.2) | collective-permute-done | bytes 458784 | tf_op jit(solution)/shard_map/ppermute | solution.py:429
  47.3 1.0 copy-done
  49.1 17.3 %all_to_all.45.blocks_ref = f32[32,8,256]{2,1,0:T(8,128)S(1)} all-to-all(f32[32,8,256]{2,1,0:T(8,128)S(1)} %bitcast.12), channel_id=1, replica_groups=mesh['replica'=4,'fsdp'=16,'tensor'=8] {'replica','tensor'}, dimensions={0} | all-to-all | bytes 524288 | tf_op jit(solution)/shard_map/all_to_all | solution.py:21
  66.5 12.5 %all_to_all.46 = f32[32,8,256]{2,1,0:T(8,128)S(1)} all-to-all(f32[32,8,256]{2,1,0:T(8,128)S(1)} %sum_copies.2), channel_id=1, replica_groups=mesh['replica'=4,'fsdp'=16,'tensor'=8] {'replica','tensor'}, dimensions={0} | all-to-all | bytes 524288 | tf_op jit(solution)/shard_map/all_to_all | solution.py:21
  79.7 18.4 %all_to_all.47.blocks_ref = f32[4,256,128]{2,1,0:T(8,128)S(1)} all-to-all(f32[4,256,128]{2,1,0:T(8,128)S(1)} %bitcast.10), channel_id=1, replica_groups={{0,8,16,24},{32,40,48,56},{64,72,80,88},{96,104,112,120},{1,9,17,25},{3..., dimensions={0} | all-to-all | bytes 1048576 | tf_op jit(solution)/shard_map/all_to_all | solution.py:21
  98.1 21.6 %all_to_all.48.blocks_ref = f32[4,64,128]{2,1,0:T(8,128)S(1)} all-to-all(f32[4,64,128]{2,1,0:T(8,128)S(1)} %sum_blocks.1), channel_id=1, replica_groups={{0,32,64,96},{8,40,72,104},{16,48,80,112},{24,56,88,120},{1,33,65,97},{..., dimensions={0} | all-to-all | bytes 262144 | tf_op jit(solution)/shard_map/all_to_all | solution.py:21
  119.7 14.9 %all_to_all.49 = f32[4,64,128]{2,1,0:T(8,128)S(1)} all-to-all(f32[4,64,128]{2,1,0:T(8,128)S(1)} %sum_copies.3), channel_id=1, replica_groups={{0,32,64,96},{8,40,72,104},{16,48,80,112},{24,56,88,120},{1,33,65,97},{..., dimensions={0} | all-to-all | bytes 262144 | tf_op jit(solution)/shard_map/all_to_all | solution.py:21
  134.6 12.4 %all_to_all.50 = f32[4,256,128]{2,1,0:T(8,128)S(1)} all-to-all(f32[4,256,128]{2,1,0:T(8,128)S(1)} %broadcast_in_dim.8), channel_id=1, replica_groups={{0,8,16,24},{32,40,48,56},{64,72,80,88},{96,104,112,120},{1,9,17,25},{3..., dimensions={0} | all-to-all | bytes 1048576 | tf_op jit(solution)/shard_map/all_to_all | solution.py:21
  147.7 10.0 %all-to-all-start.7 = ((f32[8,32,256]{2,1,0:T(8,128)}), f32[8,32,256]{2,1,0:T(8,128)S(1)}, u32[]{:S(2)}, u32[]{:S(2)}) async-start(f32[8,32,256]{2,1,0:T(8,128)} %slab.1), calls=%async_computation.7 | async-start | bytes 524288 | tf_op jit(solution)/shard_map/all_to_all | solution.py:21
  157.7 1.9 collective-permute-start.5
  159.7 3.6 %collective-permute-start.4 = (f32[16,56,128]{2,1,0:T(8,128)S(1)}, f32[16,56,128]{2,1,0:T(8,128)S(1)}, u32[]{:S(2)}, u32[]{:S(2)}) collective-permute-start(f32[16,56,128]{2,1,0:T(8,128)S(1)} %raw.1.raw_ref.refs_0_), channel_id=1, source_target_pairs={{0,256},{128,384},{256,0},{384,128},{1,257},{129,385},{257,1},{385... | collective-permute-start | bytes 1376264 | tf_op jit(solution)/shard_map/ppermute | solution.py:429
  163.3 3.1 %collective-permute-start.3 = (f32[16,56,128]{2,1,0:T(8,128)S(1)}, f32[16,56,128]{2,1,0:T(8,128)S(1)}, u32[]{:S(2)}, u32[]{:S(2)}) collective-permute-start(f32[16,56,128]{2,1,0:T(8,128)S(1)} %raw.1.raw_ref.refs_0_), channel_id=1, source_target_pairs={{0,384},{128,0},{256,128},{384,256},{1,385},{129,1},{257,129},{385... | collective-permute-start | bytes 1376264 | tf_op jit(solution)/shard_map/ppermute | solution.py:429
  166.4 10.4 %factor.1 = (f32[256,256]{1,0:T(8,128)S(1)}, f32[32,8,128]{2,1,0:T(8,128)}) custom-call(f32[256,256]{1,0:T(8,128)S(1)} %bitcast.11, f32[16,56,128]{2,1,0:T(8,128)S(1)} %raw.1.raw_ref.refs_0_), custom_call_target="tpu_custom_call" | custom-call | flops 30000001024 | bytes 1000000 | tf_op jit(solution)/shard_map/factor/pallas_call | solution.py:310
  176.7 7.9 %all-to-all-start.8 = ((f32[32,8,128]{2,1,0:T(8,128)}), f32[32,8,128]{2,1,0:T(8,128)S(1)}, u32[]{:S(2)}, u32[]{:S(2)}) async-start(f32[32,8,128]{2,1,0:T(8,128)} %get-tuple-element.29), calls=%async_computation.8 | async-start | bytes 262144 | tf_op jit(solution)/shard_map/all_to_all | solution.py:21
  184.6 1.3 combine.1
  185.9 5.0 %update.1 = (f32[1,256,1792]{2,1,0:T(8,128)}, f32[112,256]{1,0:T(8,128)S(1)}) custom-call(f32[1,256,1792]{2,1,0:T(8,128)} %get-tuple-element.26.buffer_ref, f32[256,256]{1,0:T(8,128)S(1)} %get-tuple-element.27.ortho_ref, f32[256,256]{1,0:T(8,128)S(1)} %get-tuple-element.24.inverse_ref, ...), custom_call_target="tpu_custom_call", output_to_operand_aliasing={{0}: (0, {})} | custom-call | tf_op jit(solution)/shard_map/update/pallas_call | solution.py:375
  190.9 1.4 all-to-all-done.8.squares_ref
  (15 shorter events, 3.1 us)
Async XLA Ops:
  4.4 42.9 %all-to-all-start = ((f32[16,56,128]{2,1,0:T(8,128)}), f32[16,56,128]{2,1,0:T(8,128)S(1)}, u32[]{:S(2)}, u32[]{:S(2)}) async-start(f32[16,56,128]{2,1,0:T(8,128)} %get-tuple-element.21), calls=%async_computation | async-start | bytes 917504 | tf_op jit(solution)/shard_map/all_to_all | solution.py:21
  20.1 14.4 %collective-permute-start = (f32[16,56,128]{2,1,0:T(8,128)}, f32[16,56,128]{2,1,0:T(8,128)S(1)}, u32[]{:S(2)}, u32[]{:S(2)}) collective-permute-start(f32[16,56,128]{2,1,0:T(8,128)} %get-tuple-element.18), channel_id=1, source_target_pairs={{0,128},{128,256},{256,384},{384,0},{1,129},{129,257},{257,385},{3... | collective-permute-start | bytes 1376264 | tf_op jit(solution)/shard_map/ppermute | solution.py:429
  23.3 22.1 %collective-permute-start.1 = (f32[16,56,128]{2,1,0:T(8,128)}, f32[16,56,128]{2,1,0:T(8,128)S(1)}, u32[]{:S(2)}, u32[]{:S(2)}) collective-permute-start(f32[16,56,128]{2,1,0:T(8,128)} %get-tuple-element.19), channel_id=1, source_target_pairs={{0,256},{128,384},{256,0},{384,128},{1,257},{129,385},{257,1},{385... | collective-permute-start | bytes 1376264 | tf_op jit(solution)/shard_map/ppermute | solution.py:429
  27.6 19.7 %collective-permute-start.2 = (f32[16,56,128]{2,1,0:T(8,128)}, f32[16,56,128]{2,1,0:T(8,128)S(1)}, u32[]{:S(2)}, u32[]{:S(2)}) collective-permute-start(f32[16,56,128]{2,1,0:T(8,128)} %get-tuple-element.20), channel_id=1, source_target_pairs={{0,384},{128,0},{256,128},{384,256},{1,385},{129,1},{257,129},{385... | collective-permute-start | bytes 1376264 | tf_op jit(solution)/shard_map/ppermute | solution.py:429
  47.3 1.0 copy-start
  147.7 18.7 %all-to-all-start.7 = ((f32[8,32,256]{2,1,0:T(8,128)}), f32[8,32,256]{2,1,0:T(8,128)S(1)}, u32[]{:S(2)}, u32[]{:S(2)}) async-start(f32[8,32,256]{2,1,0:T(8,128)} %slab.1), calls=%async_computation.7 | async-start | bytes 524288 | tf_op jit(solution)/shard_map/all_to_all | solution.py:21
  157.7 28.2 %collective-permute-start.5 = (f32[16,56,128]{2,1,0:T(8,128)S(1)}, f32[16,56,128]{2,1,0:T(8,128)S(1)}, u32[]{:S(2)}, u32[]{:S(2)}) collective-permute-start(f32[16,56,128]{2,1,0:T(8,128)S(1)} %raw.1.raw_ref.refs_0_), channel_id=1, source_target_pairs={{0,128},{128,256},{256,384},{384,0},{1,129},{129,257},{257,385},{3... | collective-permute-start | bytes 1376264 | tf_op jit(solution)/shard_map/ppermute | solution.py:429
  159.7 26.3 %collective-permute-start.4 = (f32[16,56,128]{2,1,0:T(8,128)S(1)}, f32[16,56,128]{2,1,0:T(8,128)S(1)}, u32[]{:S(2)}, u32[]{:S(2)}) collective-permute-start(f32[16,56,128]{2,1,0:T(8,128)S(1)} %raw.1.raw_ref.refs_0_), channel_id=1, source_target_pairs={{0,256},{128,384},{256,0},{384,128},{1,257},{129,385},{257,1},{385... | collective-permute-start | bytes 1376264 | tf_op jit(solution)/shard_map/ppermute | solution.py:429
  163.3 22.6 %collective-permute-start.3 = (f32[16,56,128]{2,1,0:T(8,128)S(1)}, f32[16,56,128]{2,1,0:T(8,128)S(1)}, u32[]{:S(2)}, u32[]{:S(2)}) collective-permute-start(f32[16,56,128]{2,1,0:T(8,128)S(1)} %raw.1.raw_ref.refs_0_), channel_id=1, source_target_pairs={{0,384},{128,0},{256,128},{384,256},{1,385},{129,1},{257,129},{385... | collective-permute-start | bytes 1376264 | tf_op jit(solution)/shard_map/ppermute | solution.py:429
  176.7 15.6 %all-to-all-start.8 = ((f32[32,8,128]{2,1,0:T(8,128)}), f32[32,8,128]{2,1,0:T(8,128)S(1)}, u32[]{:S(2)}, u32[]{:S(2)}) async-start(f32[32,8,128]{2,1,0:T(8,128)} %get-tuple-element.29), calls=%async_computation.8 | async-start | bytes 262144 | tf_op jit(solution)/shard_map/all_to_all | solution.py:21

commit v5 on v4

--- a/solution.py
+++ b/solution.py
@@ -90,15 +90,33 @@
     )(momentum, gradient, right_in)
 
 
+def own_kernel(part_ref, out_ref):
+    blocks, packed = part_ref.shape[:2]
+    piece = packed // 2
+    for block in range(blocks):
+        out_ref[block * piece : (block + 1) * piece, :] = unpack(part_ref[block])
+
+
+def unpack_own(part):
+    blocks, packed, _ = part.shape
+    return pl.pallas_call(
+        own_kernel,
+        out_shape=jax.ShapeDtypeStruct((blocks * packed // 2, 2 * LANES), jnp.float32),
+        compiler_params=pltpu.CompilerParams(vmem_limit_bytes=VMEM_LIMIT),
+        cost_estimate=pl.CostEstimate(flops=10**9, bytes_accessed=10**6, transcendentals=0),
+        name="own",
+    )(part)
+
+
 def project_kernel(part_refs, right_ref, sum_ref, out_ref, right):
     blocks, packed = right_ref.shape[:2]
     piece = packed // 2
     for block in range(blocks):
-        total = part_refs[0][block]
+        rows = slice(block * piece, (block + 1) * piece)
+        total = part_refs[0][rows, :]
         for part_ref in part_refs[1:]:
-            total = total + part_ref[block]
-        rows = slice(block * piece, (block + 1) * piece)
-        sum_ref[rows, :] = unpack(total)
+            total = total + unpack(part_ref[block])
+        sum_ref[rows, :] = total
         right[rows, :] = unpack(right_ref[block])
     out_ref[...] = column_dot(sum_ref[...], right[...])
 
@@ -430,7 +448,7 @@
 
     *turned, right_copies, buffer = turn(momentum, gradient, right_in, replicas, fsdp_count)
     right_quarter = exchange(right_copies, "fsdp")
-    parts = [turned[0]] + [around(turned[step], step) for step in range(1, replicas)]
+    parts = [unpack_own(turned[0])] + [around(turned[step], step) for step in range(1, replicas)]
     column_sum, partial_value = project(parts, right_quarter)
 
     partial_value = exchange(partial_value.reshape(group_count, band, rank), GROUP)

time: 194 us -> 193 us (level)
  no operation moved by 1% of the time
where the time goes in v5:
time: 193 us; the launch traced here: 192 us
  blocking collectives  97 us (50%)
  starting transfers between devices  52.7 us (27%)
  Pallas kernels  23.6 us (12%)
  waiting for transfers between devices  17 us (9%)
    all_to_all x6, blocking collectives, exchange(): lax.all_to_all(blocks, axes, 0, 0, tiled=True, axis_index_groups=groups)  97 us
    all_to_all x3, starting transfers between devices, exchange(): lax.all_to_all(blocks, axes, 0, 0, tiled=True, axis_index_groups=groups)  33.6 us
    ppermute x6, starting transfers between devices, around(): return lax.ppermute(value, 'replica', pairs)  19.2 us
    ppermute x6, waiting for transfers between devices, around(): return lax.ppermute(value, 'replica', pairs)  15.5 us
    pallas_call x1, Pallas kernels, make_factor(): pl.pallas_call(functools.partial(factor_kernel, replicas), out_shape=[jax...  10.4 us
    pallas_call x1, Pallas kernels, update(): pl.pallas_call(update_kernel, grid=(steps,), in_specs=[columns, pl.BlockS...  4.97 us
  transfers between devices with their start and end apart: 9, of which 4 were waited for; matrix products, arithmetic and copies ran while one was open for 0% of the time, Pallas kernels for 9%

profile of v5, /device:TPU:1, one launch (start us, length us, event | category | flops | bytes accessed | tf_op | source)
XLA Modules:
  0.0 192.1 jit_solution(13984305179346753118)
XLA Ops:
  0.6 3.7 %turn.1 = (f32[16,56,128]{2,1,0:T(8,128)}, f32[16,56,128]{2,1,0:T(8,128)}, f32[16,56,128]{2,1,0:T(8,128)}, f32[16,56,128]{2,1,0:T(8,128)}, f32[16,56,128]{2,1,0:T(8,128)}, /*index=5*/f32[1,256,1792]{2,1,0:T(8,128)}) custom-call(f32[1,256,1792]{2,1,0:T(8,128)} %momentum_ref.1, bf16[1,256,1792]{2,1,0:T(8,128)(2,1)} %gradient_ref.1, f32[112,256]{1,0:T(8,128)} %right_ref.1), custom_call_target="tpu_custom_call" | custom-call | tf_op jit(solution)/shard_map/turn/pallas_call | solution.py:79
  4.4 15.7 %all-to-all-start = ((f32[16,56,128]{2,1,0:T(8,128)}), f32[16,56,128]{2,1,0:T(8,128)S(1)}, u32[]{:S(2)}, u32[]{:S(2)}) async-start(f32[16,56,128]{2,1,0:T(8,128)} %get-tuple-element.21), calls=%async_computation | async-start | bytes 917504 | tf_op jit(solution)/shard_map/all_to_all | solution.py:21
  20.1 3.1 %collective-permute-start = (f32[16,56,128]{2,1,0:T(8,128)}, f32[16,56,128]{2,1,0:T(8,128)S(1)}, u32[]{:S(2)}, u32[]{:S(2)}) collective-permute-start(f32[16,56,128]{2,1,0:T(8,128)} %get-tuple-element.18), channel_id=1, source_target_pairs={{0,128},{128,256},{256,384},{384,0},{1,129},{129,257},{257,385},{3... | collective-permute-start | bytes 1376264 | tf_op jit(solution)/shard_map/ppermute | solution.py:447
  23.3 4.4 %collective-permute-start.1 = (f32[16,56,128]{2,1,0:T(8,128)}, f32[16,56,128]{2,1,0:T(8,128)S(1)}, u32[]{:S(2)}, u32[]{:S(2)}) collective-permute-start(f32[16,56,128]{2,1,0:T(8,128)} %get-tuple-element.19), channel_id=1, source_target_pairs={{0,256},{128,384},{256,0},{384,128},{1,257},{129,385},{257,1},{385... | collective-permute-start | bytes 1376264 | tf_op jit(solution)/shard_map/ppermute | solution.py:447
  27.6 3.1 %collective-permute-start.2 = (f32[16,56,128]{2,1,0:T(8,128)}, f32[16,56,128]{2,1,0:T(8,128)S(1)}, u32[]{:S(2)}, u32[]{:S(2)}) collective-permute-start(f32[16,56,128]{2,1,0:T(8,128)} %get-tuple-element.20), channel_id=1, source_target_pairs={{0,384},{128,0},{256,128},{384,256},{1,385},{129,1},{257,129},{385... | collective-permute-start | bytes 1376264 | tf_op jit(solution)/shard_map/ppermute | solution.py:447
  30.7 1.0 copy-done
  31.8 2.8 %collective-permute-done.refs_1_ = f32[16,56,128]{2,1,0:T(8,128)S(1)} collective-permute-done((f32[16,56,128]{2,1,0:T(8,128)}, f32[16,56,128]{2,1,0:T(8,128)S(1)}, u32[]{:S(2)}, u32[]{:S(2)}) %collective-permute-start) | collective-permute-done | bytes 458784 | tf_op jit(solution)/shard_map/ppermute | solution.py:447
  34.5 10.8 %collective-permute-done.1.refs_2_ = f32[16,56,128]{2,1,0:T(8,128)S(1)} collective-permute-done((f32[16,56,128]{2,1,0:T(8,128)}, f32[16,56,128]{2,1,0:T(8,128)S(1)}, u32[]{:S(2)}, u32[]{:S(2)}) %collective-permute-start.1) | collective-permute-done | bytes 458784 | tf_op jit(solution)/shard_map/ppermute | solution.py:447
  45.3 2.0 %collective-permute-done.2.refs_3_ = f32[16,56,128]{2,1,0:T(8,128)S(1)} collective-permute-done((f32[16,56,128]{2,1,0:T(8,128)}, f32[16,56,128]{2,1,0:T(8,128)S(1)}, u32[]{:S(2)}, u32[]{:S(2)}) %collective-permute-start.2) | collective-permute-done | bytes 458784 | tf_op jit(solution)/shard_map/ppermute | solution.py:447
  48.2 17.3 %all_to_all.45.blocks_ref = f32[32,8,256]{2,1,0:T(8,128)S(1)} all-to-all(f32[32,8,256]{2,1,0:T(8,128)S(1)} %bitcast.12), channel_id=1, replica_groups=mesh['replica'=4,'fsdp'=16,'tensor'=8] {'replica','tensor'}, dimensions={0} | all-to-all | bytes 524288 | tf_op jit(solution)/shard_map/all_to_all | solution.py:21
  65.6 12.5 %all_to_all.46 = f32[32,8,256]{2,1,0:T(8,128)S(1)} all-to-all(f32[32,8,256]{2,1,0:T(8,128)S(1)} %sum_copies.2), channel_id=1, replica_groups=mesh['replica'=4,'fsdp'=16,'tensor'=8] {'replica','tensor'}, dimensions={0} | all-to-all | bytes 524288 | tf_op jit(solution)/shard_map/all_to_all | solution.py:21
  78.8 18.4 %all_to_all.47.blocks_ref = f32[4,256,128]{2,1,0:T(8,128)S(1)} all-to-all(f32[4,256,128]{2,1,0:T(8,128)S(1)} %bitcast.10), channel_id=1, replica_groups={{0,8,16,24},{32,40,48,56},{64,72,80,88},{96,104,112,120},{1,9,17,25},{3..., dimensions={0} | all-to-all | bytes 1048576 | tf_op jit(solution)/shard_map/all_to_all | solution.py:21
  97.2 21.6 %all_to_all.48.blocks_ref = f32[4,64,128]{2,1,0:T(8,128)S(1)} all-to-all(f32[4,64,128]{2,1,0:T(8,128)S(1)} %sum_blocks.1), channel_id=1, replica_groups={{0,32,64,96},{8,40,72,104},{16,48,80,112},{24,56,88,120},{1,33,65,97},{..., dimensions={0} | all-to-all | bytes 262144 | tf_op jit(solution)/shard_map/all_to_all | solution.py:21
  118.7 14.9 %all_to_all.49 = f32[4,64,128]{2,1,0:T(8,128)S(1)} all-to-all(f32[4,64,128]{2,1,0:T(8,128)S(1)} %sum_copies.3), channel_id=1, replica_groups={{0,32,64,96},{8,40,72,104},{16,48,80,112},{24,56,88,120},{1,33,65,97},{..., dimensions={0} | all-to-all | bytes 262144 | tf_op jit(solution)/shard_map/all_to_all | solution.py:21
  133.7 12.4 %all_to_all.50 = f32[4,256,128]{2,1,0:T(8,128)S(1)} all-to-all(f32[4,256,128]{2,1,0:T(8,128)S(1)} %broadcast_in_dim.8), channel_id=1, replica_groups={{0,8,16,24},{32,40,48,56},{64,72,80,88},{96,104,112,120},{1,9,17,25},{3..., dimensions={0} | all-to-all | bytes 1048576 | tf_op jit(solution)/shard_map/all_to_all | solution.py:21
  146.8 10.0 %all-to-all-start.7 = ((f32[8,32,256]{2,1,0:T(8,128)}), f32[8,32,256]{2,1,0:T(8,128)S(1)}, u32[]{:S(2)}, u32[]{:S(2)}) async-start(f32[8,32,256]{2,1,0:T(8,128)} %slab.1), calls=%async_computation.7 | async-start | bytes 524288 | tf_op jit(solution)/shard_map/all_to_all | solution.py:21
  156.8 1.9 %collective-permute-start.5 = (f32[16,56,128]{2,1,0:T(8,128)S(1)}, f32[16,56,128]{2,1,0:T(8,128)S(1)}, u32[]{:S(2)}, u32[]{:S(2)}) collective-permute-start(f32[16,56,128]{2,1,0:T(8,128)S(1)} %raw.1.raw_ref.refs_0_), channel_id=1, source_target_pairs={{0,128},{128,256},{256,384},{384,0},{1,129},{129,257},{257,385},{3... | collective-permute-start | bytes 1376264 | tf_op jit(solution)/shard_map/ppermute | solution.py:447
  158.7 3.6 %collective-permute-start.4 = (f32[16,56,128]{2,1,0:T(8,128)S(1)}, f32[16,56,128]{2,1,0:T(8,128)S(1)}, u32[]{:S(2)}, u32[]{:S(2)}) collective-permute-start(f32[16,56,128]{2,1,0:T(8,128)S(1)} %raw.1.raw_ref.refs_0_), channel_id=1, source_target_pairs={{0,256},{128,384},{256,0},{384,128},{1,257},{129,385},{257,1},{385... | collective-permute-start | bytes 1376264 | tf_op jit(solution)/shard_map/ppermute | solution.py:447
  162.4 3.1 %collective-permute-start.3 = (f32[16,56,128]{2,1,0:T(8,128)S(1)}, f32[16,56,128]{2,1,0:T(8,128)S(1)}, u32[]{:S(2)}, u32[]{:S(2)}) collective-permute-start(f32[16,56,128]{2,1,0:T(8,128)S(1)} %raw.1.raw_ref.refs_0_), channel_id=1, source_target_pairs={{0,384},{128,0},{256,128},{384,256},{1,385},{129,1},{257,129},{385... | collective-permute-start | bytes 1376264 | tf_op jit(solution)/shard_map/ppermute | solution.py:447
  165.4 10.4 %factor.1 = (f32[256,256]{1,0:T(8,128)S(1)}, f32[32,8,128]{2,1,0:T(8,128)}) custom-call(f32[256,256]{1,0:T(8,128)S(1)} %bitcast.11, f32[16,56,128]{2,1,0:T(8,128)S(1)} %raw.1.raw_ref.refs_0_), custom_call_target="tpu_custom_call" | custom-call | flops 30000001024 | bytes 1000000 | tf_op jit(solution)/shard_map/factor/pallas_call | solution.py:328
  175.8 7.9 %all-to-all-start.8 = ((f32[32,8,128]{2,1,0:T(8,128)}), f32[32,8,128]{2,1,0:T(8,128)S(1)}, u32[]{:S(2)}, u32[]{:S(2)}) async-start(f32[32,8,128]{2,1,0:T(8,128)} %get-tuple-element.29), calls=%async_computation.8 | async-start | bytes 262144 | tf_op jit(solution)/shard_map/all_to_all | solution.py:21
  183.7 1.3 combine.1
  185.0 5.0 %update.1 = (f32[1,256,1792]{2,1,0:T(8,128)}, f32[112,256]{1,0:T(8,128)S(1)}) custom-call(f32[1,256,1792]{2,1,0:T(8,128)} %get-tuple-element.26.buffer_ref, f32[256,256]{1,0:T(8,128)S(1)} %get-tuple-element.27.ortho_ref, f32[256,256]{1,0:T(8,128)S(1)} %get-tuple-element.24.inverse_ref, ...), custom_call_target="tpu_custom_call", output_to_operand_aliasing={{0}: (0, {})} | custom-call | tf_op jit(solution)/shard_map/update/pallas_call | solution.py:393
  190.0 1.4 all-to-all-done.8.squares_ref
  (16 shorter events, 3.3 us)
Async XLA Ops:
  4.4 42.9 %all-to-all-start = ((f32[16,56,128]{2,1,0:T(8,128)}), f32[16,56,128]{2,1,0:T(8,128)S(1)}, u32[]{:S(2)}, u32[]{:S(2)}) async-start(f32[16,56,128]{2,1,0:T(8,128)} %get-tuple-element.21), calls=%async_computation | async-start | bytes 917504 | tf_op jit(solution)/shard_map/all_to_all | solution.py:21
  20.1 14.4 %collective-permute-start = (f32[16,56,128]{2,1,0:T(8,128)}, f32[16,56,128]{2,1,0:T(8,128)S(1)}, u32[]{:S(2)}, u32[]{:S(2)}) collective-permute-start(f32[16,56,128]{2,1,0:T(8,128)} %get-tuple-element.18), channel_id=1, source_target_pairs={{0,128},{128,256},{256,384},{384,0},{1,129},{129,257},{257,385},{3... | collective-permute-start | bytes 1376264 | tf_op jit(solution)/shard_map/ppermute | solution.py:447
  23.3 22.1 %collective-permute-start.1 = (f32[16,56,128]{2,1,0:T(8,128)}, f32[16,56,128]{2,1,0:T(8,128)S(1)}, u32[]{:S(2)}, u32[]{:S(2)}) collective-permute-start(f32[16,56,128]{2,1,0:T(8,128)} %get-tuple-element.19), channel_id=1, source_target_pairs={{0,256},{128,384},{256,0},{384,128},{1,257},{129,385},{257,1},{385... | collective-permute-start | bytes 1376264 | tf_op jit(solution)/shard_map/ppermute | solution.py:447
  27.6 19.7 %collective-permute-start.2 = (f32[16,56,128]{2,1,0:T(8,128)}, f32[16,56,128]{2,1,0:T(8,128)S(1)}, u32[]{:S(2)}, u32[]{:S(2)}) collective-permute-start(f32[16,56,128]{2,1,0:T(8,128)} %get-tuple-element.20), channel_id=1, source_target_pairs={{0,384},{128,0},{256,128},{384,256},{1,385},{129,1},{257,129},{385... | collective-permute-start | bytes 1376264 | tf_op jit(solution)/shard_map/ppermute | solution.py:447
  30.7 1.0 copy-start
  146.8 18.7 %all-to-all-start.7 = ((f32[8,32,256]{2,1,0:T(8,128)}), f32[8,32,256]{2,1,0:T(8,128)S(1)}, u32[]{:S(2)}, u32[]{:S(2)}) async-start(f32[8,32,256]{2,1,0:T(8,128)} %slab.1), calls=%async_computation.7 | async-start | bytes 524288 | tf_op jit(solution)/shard_map/all_to_all | solution.py:21
  156.8 28.2 %collective-permute-start.5 = (f32[16,56,128]{2,1,0:T(8,128)S(1)}, f32[16,56,128]{2,1,0:T(8,128)S(1)}, u32[]{:S(2)}, u32[]{:S(2)}) collective-permute-start(f32[16,56,128]{2,1,0:T(8,128)S(1)} %raw.1.raw_ref.refs_0_), channel_id=1, source_target_pairs={{0,128},{128,256},{256,384},{384,0},{1,129},{129,257},{257,385},{3... | collective-permute-start | bytes 1376264 | tf_op jit(solution)/shard_map/ppermute | solution.py:447
  158.7 26.3 %collective-permute-start.4 = (f32[16,56,128]{2,1,0:T(8,128)S(1)}, f32[16,56,128]{2,1,0:T(8,128)S(1)}, u32[]{:S(2)}, u32[]{:S(2)}) collective-permute-start(f32[16,56,128]{2,1,0:T(8,128)S(1)} %raw.1.raw_ref.refs_0_), channel_id=1, source_target_pairs={{0,256},{128,384},{256,0},{384,128},{1,257},{129,385},{257,1},{385... | collective-permute-start | bytes 1376264 | tf_op jit(solution)/shard_map/ppermute | solution.py:447
  162.4 22.6 %collective-permute-start.3 = (f32[16,56,128]{2,1,0:T(8,128)S(1)}, f32[16,56,128]{2,1,0:T(8,128)S(1)}, u32[]{:S(2)}, u32[]{:S(2)}) collective-permute-start(f32[16,56,128]{2,1,0:T(8,128)S(1)} %raw.1.raw_ref.refs_0_), channel_id=1, source_target_pairs={{0,384},{128,0},{256,128},{384,256},{1,385},{129,1},{257,129},{385... | collective-permute-start | bytes 1376264 | tf_op jit(solution)/shard_map/ppermute | solution.py:447
  175.8 15.6 %all-to-all-start.8 = ((f32[32,8,128]{2,1,0:T(8,128)}), f32[32,8,128]{2,1,0:T(8,128)S(1)}, u32[]{:S(2)}, u32[]{:S(2)}) async-start(f32[32,8,128]{2,1,0:T(8,128)} %get-tuple-element.29), calls=%async_computation.8 | async-start | bytes 262144 | tf_op jit(solution)/shard_map/all_to_all | solution.py:21
